TPU v7x, 256 devices: a whole 4x4x8 slice. The times are simulated.
256 devices in a mesh: gx: 8 (over y, core), gy: 8 (over z), gz: 4 (over x).
Axes of the slice: x: 4, y: 4, z: 8, core: 2. Of those that a mesh axis runs over, the one named last changes fastest.
Arguments:
- positions: float32 [3, 65536], P(None, ('gx', 'gy', 'gz')), may hold values from 0 to 3
- features: bfloat16 [64, 65536], P(None, ('gx', 'gy', 'gz')), may hold values from -6 to 6
- ghost_rows: int32 [32768], P(('gx', 'gy', 'gz')), may hold values from 0 to 255, as said below
- pair_center: int32 [786432], P(('gx', 'gy', 'gz')), may hold values from 0 to 255, as said below
- pair_nbr: int32 [786432], P(('gx', 'gy', 'gz')), may hold values from 0 to 3711, as said below
- pair_count: int32 [256], P(('gx', 'gy', 'gz')), may hold values from 1536 to 3072, as said below
- emb_weight: float32 [136, 64], replicated, may hold values from -0.5 to 0.5
- value_weight: float32 [64, 64], replicated, may hold values from -0.75 to 0.75
- env_weight: float32 [2, 64, 64], replicated, may hold values from -0.75 to 0.75
- path_weight: float32 [2, 7, 64], replicated, may hold values from 0.5 to 1.5
- latent_weight: float32 [2, 256, 64], replicated, may hold values from -0.375 to 0.375
- gate_weight: float32 [1, 64, 64], replicated, may hold values from -0.75 to 0.75
- final_weight: float32 [64, 64], replicated, may hold values from -0.75 to 0.75
- out_weight: float32 [64], replicated, may hold values from -0.75 to 0.75
Outputs:
- site_energy: float32 [65536], P(('gx', 'gy', 'gz'))
- forces: float32 [3, 65536], P(None, ('gx', 'gy', 'gz'))
Inputs may be any that keep to these rules, and one draw needn't show every extreme that they name: `ghost_rows`: the 128 entries of one block are distinct block-local atom indices. `pair_center`: block-local atom indices. `pair_nbr`: an index below 256 is an own atom other than the center; else it is 256 + k * 128 + r with slot k never 13. `pair_count`: some block is full in every draw.
All inputs are finite; a program needn't handle non-finite values.
Results may differ from a plain program's by a relative error of at most 0.0004.
Values sent between devices are 32-bit elements; how exact they have to be, the bound alone decides.
A program may use at most 192 MiB of HBM per device.

v0:
```python
import jax
import jax.numpy as jnp
from jax import lax
from jax.sharding import PartitionSpec as P

edge_length = 3.0
env_scale = 0.125
root_three = 1.7320508075688772


def with_halo(block, sides, width):
    for axis, dim in sides:
        count = lax.axis_size(axis)
        forward = [(i, i + 1) for i in range(count - 1)]
        forward.append((count - 1, 0))
        backward = [(target, source) for source, target in forward]
        low = lax.ppermute(
            lax.slice_in_dim(block, block.shape[dim] - width, None, axis=dim), axis, forward
        )
        high = lax.ppermute(lax.slice_in_dim(block, 0, width, axis=dim), axis, backward)
        block = jnp.concatenate([low, block, high], axis=dim)
    return block


def matmul(weight, data):
    return jnp.dot(weight.T, data, precision=lax.Precision.HIGHEST)


def slot_offsets():
    slots = jnp.arange(27, dtype=jnp.int32)
    return (
        jnp.stack([slots // 9 - 1, slots // 3 % 3 - 1, slots % 3 - 1]).astype(jnp.float32)
        * edge_length
    )


def site_energies(local_pos, ghost_pos, local_feat, ghost_feat, center, neighbour, count, params):
    (
        emb_weight,
        value_weight,
        env_weight,
        path_weight,
        latent_weight,
        gate_weight,
        final_weight,
        out_weight,
    ) = params
    atoms = local_pos.shape[1]
    slots = center.shape[0]
    all_pos = jnp.concatenate([local_pos, ghost_pos], 1)
    all_feat = jnp.concatenate([local_feat, ghost_feat], 1)
    delta = all_pos[:, neighbour] - all_pos[:, center]
    radius = jnp.sqrt(jnp.sum(delta * delta, 0) + 1.0)
    unit = delta / radius
    ux, uy, uz = (unit[0], unit[1], unit[2])
    harmonic = jnp.stack(
        [
            jnp.ones_like(ux),
            ux,
            uy,
            uz,
            root_three * ux * uy,
            root_three * uy * uz,
            root_three * uz * ux,
            root_three * 0.5 * (ux * ux - uy * uy),
            0.5 * (2.0 * uz * uz - ux * ux - uy * uy),
        ]
    )
    live = (jnp.arange(slots, dtype=jnp.int32) < count).astype(jnp.float32)
    centers_mu = jnp.arange(emb_weight.shape[0] - 2 * local_feat.shape[0], dtype=jnp.float32) * 1.25
    basis = jnp.exp(-0.5 * (radius[None, :] - centers_mu[:, None]) ** 2)
    joined = jnp.concatenate([all_feat[:, center], all_feat[:, neighbour], basis], 0)
    latent = jax.nn.silu(matmul(emb_weight, joined))
    tensor = matmul(value_weight, latent)[None] * harmonic[:, None]
    layers = env_weight.shape[0]
    for layer in range(layers):
        embed = matmul(env_weight[layer], latent) * live[None]
        message = embed[None] * harmonic[:, None]
        chans = latent.shape[0]
        gamma = jnp.zeros((9, chans, atoms), jnp.float32).at[:, :, center].add(message) * env_scale
        beside_all = gamma[:, :, center]
        weights = path_weight[layer][:, :, None]
        scalar0 = tensor[0] * beside_all[0]
        scalar1 = jnp.sum(tensor[1:4] * beside_all[1:4], 0)
        scalar2 = jnp.sum(tensor[4:] * beside_all[4:], 0)
        mixed = jnp.concatenate(
            [latent, weights[0] * scalar0, weights[1] * scalar1, weights[2] * scalar2], 0
        )
        latent = latent + jax.nn.silu(matmul(latent_weight[layer], mixed))
        if layer < layers - 1:
            gating = matmul(gate_weight[layer], latent)
            part0 = (weights[0] * scalar0 + weights[1] * scalar1 + weights[2] * scalar2)[None]
            part1 = (
                weights[3] * tensor[0][None] * beside_all[1:4]
                + weights[4] * tensor[1:4] * beside_all[0][None]
            )
            part2 = (
                weights[5] * tensor[0][None] * beside_all[4:]
                + weights[6] * tensor[4:] * beside_all[0][None]
            )
            tensor = jnp.concatenate([part0, part1, part2], 0) * gating[None]
    hidden = jax.nn.silu(matmul(final_weight, latent))
    energy = jnp.dot(out_weight, hidden, precision=lax.Precision.HIGHEST) * live
    return jnp.zeros((atoms,), jnp.float32).at[center].add(energy)


def energy_grads(local_pos, ghost_pos, local_feat, ghost_feat, center, neighbour, count, params):

    def total(first, second):
        site = site_energies(
            first, second, local_feat, ghost_feat, center, neighbour, count, params
        )
        return (jnp.sum(site), site)

    value, pullback, site = jax.vjp(total, local_pos, ghost_pos, has_aux=True)
    local_grad, ghost_grad = pullback(jnp.ones((), jnp.float32))
    return (local_grad, ghost_grad, site)


def local(
    positions,
    features,
    ghost_rows,
    pair_center,
    pair_nbr,
    pair_count,
    emb_weight,
    value_weight,
    env_weight,
    path_weight,
    latent_weight,
    gate_weight,
    final_weight,
    out_weight,
):
    params = (
        emb_weight,
        value_weight,
        env_weight,
        path_weight,
        latent_weight,
        gate_weight,
        final_weight,
        out_weight,
    )
    rows_sent = ghost_rows.shape[0]
    chans = features.shape[0]
    feats = features.astype(jnp.float32)
    outgoing = jnp.concatenate([feats, positions], 0)[:, ghost_rows]
    received = with_halo(outgoing[None, None, None], (("gx", 0), ("gy", 1), ("gz", 2)), 1)
    received = received.reshape(27, chans + 3, rows_sent)
    ghost_feat = jnp.moveaxis(received[:, :chans], 0, 1).reshape(chans, 27 * rows_sent)
    ghost_pos = (jnp.moveaxis(received[:, chans:], 0, 1) + slot_offsets()[:, :, None]).reshape(
        3, 27 * rows_sent
    )
    local_grad, ghost_grad, site = energy_grads(
        positions, ghost_pos, feats, ghost_feat, pair_center, pair_nbr, pair_count[0], params
    )
    per_slot = jnp.moveaxis(ghost_grad.reshape(3, 27, rows_sent), 0, 1)
    returned = with_halo(per_slot[None, None, None], (("gx", 0), ("gy", 1), ("gz", 2)), 1)
    returned = returned.reshape(27, 27, 3, rows_sent)
    picks = jnp.arange(27, dtype=jnp.int32)
    owned = jnp.sum(returned[picks, 26 - picks], 0)
    total_grad = local_grad.at[:, ghost_rows].add(owned)
    return (site, -total_grad)


def solution(mesh):
    placed = (
        P(None, ("gx", "gy", "gz")),
        P(None, ("gx", "gy", "gz")),
        P(("gx", "gy", "gz")),
        P(("gx", "gy", "gz")),
        P(("gx", "gy", "gz")),
        P(("gx", "gy", "gz")),
        P(),
        P(),
        P(),
        P(),
        P(),
        P(),
        P(),
        P(),
    )
    return jax.shard_map(
        local,
        mesh=mesh,
        in_specs=placed,
        out_specs=(P(("gx", "gy", "gz")), P(None, ("gx", "gy", "gz"))),
        check_vma=False,
    )
```

profile of v0, /device:TPU:1, one launch (start us, length us, event | category | flops | bytes accessed | tf_op | source)
XLA Modules:
  0.0 1546.1 jit_solution(5251424093793814041)
XLA Ops:
  13.2 19.4 %gather_fusion.7 = f32[3072]{0:T(1024)S(1)} fusion(f32[256]{0:T(256)S(1)} %broadcast_in_dim.43, s32[3072]{0:T(1024)S(1)} %get-tuple-element.76), kind=kCustom, calls=%fused_computation.7 | custom fusion | bytes 36864 | tf_op jit(solution)/shard_map/transpose(jvp())/gather | solution.py:104
  57.4 12.3 gather_fusion.4
  69.8 9.6 gather_fusion.3
  81.0 11.9 gather_fusion.1
  92.9 11.8 gather_fusion.2
  124.0 18.4 %copy.208 = f32[3072,9,64]{2,1,0:T(8,128)} copy(f32[3072,9,64]{0,2,1:T(8,128)} %get-tuple-element.65) | data formatting | bytes 14155776 | tf_op jit(solution)/shard_map/jvp()/mul | solution.py:78
  142.6 237.9 %scatter_fusion = f32[9,64,256]{1,0,2:T(8,128)S(1)} fusion(f32[9,64,256]{1,0,2:T(8,128)S(1)} %broadcast.486.clone, s32[3072]{0:T(1024)S(1)} %copy-done.35, f32[3072,9,64]{2,1,0:T(8,128)} %copy.208), kind=kCustom, calls=%fused_computation.11 | custom fusion | flops 1769472 | bytes 21245952 | tf_op jit(solution)/shard_map/jvp()/scatter-add | solution.py:80
  381.9 29.3 %gather_fusion.5 = f32[3072,9,64]{2,1,0:T(8,128)} fusion(f32[9,64,256]{1,0,2:T(8,128)} %broadcast_multiply_fusion.4, s32[3072]{0:T(1024)S(1)} %get-tuple-element.76), kind=kCustom, calls=%fused_computation.5 | custom fusion | bytes 14168064 | tf_op jit(solution)/shard_map/jvp()/gather | solution.py:81
  411.2 17.3 %copy.209 = f32[3072,9,64]{0,2,1:T(8,128)} copy(f32[3072,9,64]{2,1,0:T(8,128)} %gather_fusion.5) | data formatting | bytes 14155776 | tf_op jit(solution)/shard_map/jvp()/gather | solution.py:81
  453.8 18.4 %copy.210 = f32[3072,9,64]{2,1,0:T(8,128)} copy(f32[3072,9,64]{0,2,1:T(8,128)} %multiply_bitcast_fusion) | data formatting | bytes 14155776 | tf_op jit(solution)/shard_map/jvp()/mul | solution.py:78
  472.4 237.9 %scatter_fusion.1 = f32[9,64,256]{1,0,2:T(8,128)S(1)} fusion(f32[9,64,256]{1,0,2:T(8,128)S(1)} %broadcast.486.clone.1, s32[3072]{0:T(1024)S(1)} %copy-done.35, f32[3072,9,64]{2,1,0:T(8,128)} %copy.210), kind=kCustom, calls=%fused_computation.12 | custom fusion | flops 1769472 | bytes 21245952 | tf_op jit(solution)/shard_map/jvp()/scatter-add | solution.py:80
  711.7 29.3 %gather_fusion.6 = f32[3072,9,64]{2,1,0:T(8,128)} fusion(f32[9,64,256]{1,0,2:T(8,128)} %broadcast_multiply_fusion.3, s32[3072]{0:T(1024)S(1)} %get-tuple-element.76), kind=kCustom, calls=%fused_computation.6 | custom fusion | bytes 14168064 | tf_op jit(solution)/shard_map/jvp()/gather | solution.py:81
  741.1 17.0 %copy.211 = f32[3072,9,64]{0,2,1:T(8,128)} copy(f32[3072,9,64]{2,1,0:T(8,128)} %gather_fusion.6) | data formatting | bytes 14155776 | tf_op jit(solution)/shard_map/jvp()/gather | solution.py:81
  784.7 18.4 %copy.212 = f32[3072,9,64]{2,1,0:T(8,128)} copy(f32[3072,9,64]{0,2,1:T(8,128)} %add_bitcast_fusion.1) | data formatting | bytes 14155776 | tf_op jit(solution)/shard_map/transpose(jvp())/add_any | solution.py:83
  803.3 237.9 %scatter_fusion.2 = f32[9,64,256]{1,0,2:T(8,128)S(1)} fusion(f32[9,64,256]{1,0,2:T(8,128)S(1)} %broadcast.486.clone.2, s32[3072]{0:T(1024)S(1)} %copy-done.35, f32[3072,9,64]{2,1,0:T(8,128)} %copy.212), kind=kCustom, calls=%fused_computation.14 | custom fusion | flops 1769472 | bytes 21245952 | tf_op jit(solution)/shard_map/transpose(jvp())/scatter-add | solution.py:81
  1042.6 29.5 %gather_fusion.8 = f32[3072,9,64]{2,1,0:T(8,128)} fusion(f32[9,64,256]{1,0,2:T(8,128)} %broadcast_multiply_fusion.2, s32[3072]{0:T(1024)S(1)} %get-tuple-element.76), kind=kCustom, calls=%fused_computation.8 | custom fusion | bytes 14168064 | tf_op jit(solution)/shard_map/transpose(jvp())/gather | solution.py:80
  1072.2 17.0 %copy.213 = f32[3072,9,64]{0,2,1:T(8,128)} copy(f32[3072,9,64]{2,1,0:T(8,128)} %gather_fusion.8) | data formatting | bytes 14155776 | tf_op jit(solution)/shard_map/transpose(jvp())/gather | solution.py:80
  1135.4 18.7 %copy.214 = f32[3072,9,64]{2,1,0:T(8,128)} copy(f32[3072,9,64]{0,2,1:T(8,128)} %add_bitcast_fusion) | data formatting | bytes 14155776 | tf_op jit(solution)/shard_map/transpose(jvp())/add_any | solution.py:83
  1154.3 237.9 %scatter_fusion.3 = f32[9,64,256]{1,0,2:T(8,128)S(1)} fusion(f32[9,64,256]{1,0,2:T(8,128)S(1)} %broadcast.486, s32[3072]{0:T(1024)S(1)} %copy-done.35, f32[3072,9,64]{2,1,0:T(8,128)} %copy.214), kind=kCustom, calls=%fused_computation.15 | custom fusion | flops 1769472 | bytes 21245952 | tf_op jit(solution)/shard_map/transpose(jvp())/scatter-add | solution.py:81
  1393.7 29.3 %gather_fusion.9 = f32[3072,9,64]{2,1,0:T(8,128)} fusion(f32[9,64,256]{1,0,2:T(8,128)} %broadcast_multiply_fusion.1, s32[3072]{0:T(1024)S(1)} %get-tuple-element.76), kind=kCustom, calls=%fused_computation.9 | custom fusion | bytes 14168064 | tf_op jit(solution)/shard_map/transpose(jvp())/gather | solution.py:80
  1423.0 17.0 %copy.215 = f32[3072,9,64]{0,2,1:T(8,128)} copy(f32[3072,9,64]{2,1,0:T(8,128)} %gather_fusion.9) | data formatting | bytes 14155776 | tf_op jit(solution)/shard_map/transpose(jvp())/gather | solution.py:80
  1456.3 18.4 %scatter_custom_fusion.6 = f32[3,3712]{0,1:T(8,128)} fusion(s32[3072]{0:T(1024)} %get-tuple-element.71, f32[3072,3]{1,0:T(8,128)S(1)} %copy.217, f32[]{:T(128)} %constant.28.clone.1), kind=kCustom, calls=%fused_computation.116 | custom fusion | flops 9216 | bytes 45056 | tf_op jit(solution)/shard_map/transpose(jvp())/scatter-add | solution.py:52
  1474.7 18.5 %scatter_custom_fusion.5 = f32[3,3712]{0,1:T(8,128)} fusion(s32[3072]{0:T(1024)} %get-tuple-element.75, f32[3072,3]{1,0:T(8,128)S(1)} %copy.216, f32[]{:T(128)} %constant.28.clone.1), kind=kCustom, calls=%fused_computation.118 | custom fusion | flops 9216 | bytes 45056 | tf_op jit(solution)/shard_map/transpose(jvp())/scatter-add | solution.py:52
  1519.3 22.3 %scatter_custom_fusion.2 = f32[256]{0:T(256)} fusion(s32[3072]{0:T(1024)S(1)} %copy-done.35, f32[3072]{0:T(1024)S(1)} %fusion.108, f32[]{:T(128)} %constant.28.clone.1), kind=kCustom, calls=%fused_computation.308 | custom fusion | flops 3072 | bytes 1028 | tf_op jit(solution)/shard_map/jvp()/scatter-add | solution.py:104
  (323 shorter events, 207.7 us)
Async XLA Ops:
  0.6 107.9 %copy-start = (f32[136,64]{0,1:T(8,128)S(1)}, f32[136,64]{0,1:T(8,128)}, u32[]{:S(2)}) copy-start(f32[136,64]{0,1:T(8,128)} %param.20) | copy-start | bytes 104452
  1.6 31.1 %copy-start.27 = (f32[64,256]{0,1:T(8,128)}, f32[64,256]{0,1:T(8,128)S(1)}, u32[]{:S(2)}) copy-start(f32[64,256]{0,1:T(8,128)S(1)} %convert_element_type.17) | copy-start | bytes 196612
  4.4 28.2 %collective-permute-start = (f32[1,1,1,67,128]{3,4,2,1,0:T(8,128)S(1)}, f32[1,1,1,67,128]{3,4,2,1,0:T(8,128)S(1)}, u32[]{:S(2)}, u32[]{:S(2)}) collective-permute-start(f32[1,1,1,67,128]{3,4,2,1,0:T(8,128)S(1)} %bitcast.268), channel_id=1, source_target_pairs={{0,32},{32,64},{64,96},{96,128},{128,160},{160,192},{192,224},{224... | collective-permute-start | bytes 102920 | tf_op jit(solution)/shard_map/ppermute | solution.py:17
  7.1 25.5 %collective-permute-start.1 = (f32[1,1,1,67,128]{3,4,2,1,0:T(8,128)S(1)}, f32[1,1,1,67,128]{3,4,2,1,0:T(8,128)S(1)}, u32[]{:S(2)}, u32[]{:S(2)}) collective-permute-start(f32[1,1,1,67,128]{3,4,2,1,0:T(8,128)S(1)} %bitcast.269), channel_id=1, source_target_pairs={{32,0},{64,32},{96,64},{128,96},{160,128},{192,160},{224,192},{0,2... | collective-permute-start | bytes 102920 | tf_op jit(solution)/shard_map/ppermute | solution.py:20
  13.2 31.9 %copy-start.49 = (s32[3072]{0:T(1024)S(1)}, s32[3072]{0:T(1024)}, u32[]{:S(2)}) copy-start(s32[3072]{0:T(1024)} %param.17) | copy-start | bytes 36868
  32.7 8.5 collective-permute-start.2
  33.8 7.4 collective-permute-start.3
  41.5 7.7 collective-permute-start.4
  42.8 6.6 collective-permute-start.5
  50.8 19.0 %copy-start.46 = (s32[3072]{0:T(1024)S(1)}, s32[3072]{0:T(1024)}, u32[]{:S(2)}) copy-start(s32[3072]{0:T(1024)} %get-tuple-element.72) | copy-start | bytes 36868
  124.0 18.5 %copy-start.35 = (s32[3072]{0:T(1024)S(1)}, s32[3072]{0:T(1024)}, u32[]{:S(2)}) copy-start(s32[3072]{0:T(1024)} %get-tuple-element.78) | copy-start | bytes 36868
  411.2 18.5 %copy-start.56 = (f32[64]{0:T(128)S(1)}, f32[64]{0:T(128)}, u32[]{:S(2)}) copy-start(f32[64]{0:T(128)} %get-tuple-element.86) | copy-start | bytes 772
  1072.2 24.8 %copy-start.10 = (f32[3,64,3072]{2,1,0:T(8,128)S(1)}, f32[3,64,3072]{2,1,0:T(8,128)}, u32[]{:S(2)}) copy-start(f32[3,64,3072]{2,1,0:T(8,128)} %get-tuple-element.60) | copy-start | bytes 7077892
  1423.0 18.5 %copy-start.9 = (f32[3,64,3072]{2,1,0:T(8,128)S(1)}, f32[3,64,3072]{2,1,0:T(8,128)}, u32[]{:S(2)}) copy-start(f32[3,64,3072]{2,1,0:T(8,128)} %get-tuple-element.45) | copy-start | bytes 7077892
  1495.5 19.2 %copy-start.11 = (f32[3,3712]{0,1:T(8,128)}, f32[3,3712]{0,1:T(8,128)S(1)}, u32[]{:S(2)}) copy-start(f32[3,3712]{0,1:T(8,128)S(1)} %add_any.228) | copy-start | bytes 133636
  1495.5 21.9 %copy-start.75 = (f32[64]{0:T(128)S(1)}, f32[64]{0:T(128)}, u32[]{:S(2)}) copy-start(f32[64]{0:T(128)} %param.27) | copy-start | bytes 772
  1499.1 7.0 collective-permute-start.6
  1505.0 3.4 collective-permute-start.7
  1508.5 5.8 collective-permute-start.8
  1508.6 5.7 collective-permute-start.9
  1514.7 26.9 %collective-permute-start.10 = (f32[3,3,1,27,3,128]{5,2,4,3,1,0:T(1,128)S(1)}, f32[3,3,1,27,3,128]{5,2,4,3,1,0:T(1,128)S(1)}, u32[]{:S(2)}, u32[]{:S(2)}) collective-permute-start(f32[3,3,1,27,3,128]{5,2,4,3,1,0:T(1,128)S(1)} %pad_maximum_fusion.5), channel_id=1, source_target_pairs={{0,1},{1,2},{2,3},{3,0},{4,5},{5,6},{6,7},{7,4},{8,9},{9,10},{10,1... | collective-permute-start | bytes 1119752 | tf_op jit(solution)/shard_map/ppermute | solution.py:17
  1515.8 25.7 %collective-permute-start.11 = (f32[3,3,1,27,3,128]{5,2,4,3,1,0:T(1,128)S(1)}, f32[3,3,1,27,3,128]{5,2,4,3,1,0:T(1,128)S(1)}, u32[]{:S(2)}, u32[]{:S(2)}) collective-permute-start(f32[3,3,1,27,3,128]{5,2,4,3,1,0:T(1,128)S(1)} %pad_maximum_fusion.5), channel_id=1, source_target_pairs={{1,0},{2,1},{3,2},{0,3},{5,4},{6,5},{7,6},{4,7},{9,8},{10,9},{11,1... | collective-permute-start | bytes 1119752 | tf_op jit(solution)/shard_map/ppermute | solution.py:20
  1519.2 24.6 %slice-start.6 = ((f32[3,3712]{0,1:T(8,128)}), f32[3,256]{0,1:T(8,128)S(1)}, s32[]{:S(2)}) async-start(f32[3,3712]{0,1:T(8,128)} %copy-done.11), calls=%async_computation.6 | async-start | bytes 262144 | tf_op jit(solution)/shard_map/transpose(jvp())/split | solution.py:50
  1519.2 24.6 %copy-start.72 = (s32[128]{0:T(128)S(1)}, s32[128]{0:T(128)}, u32[]{:S(2)}) copy-start(s32[128]{0:T(128)} %copy-done.71) | copy-start | bytes 1540
  (76 other events, 428.0 us)
where the time goes:
time: 1570 us; the launch traced here: 1550 us
  other arithmetic  1120 us (71%)
  local copies, waits for them, and re-layouts  350 us (22%)
  matrix products  33.8 us (2%)
  starting transfers between devices  23 us (1%)
    scatter-add x2, other arithmetic, site_energies(): beside_all = gamma[:, :, center]  476 us
    scatter-add x2, other arithmetic, site_energies(): jnp.zeros((9, chans, atoms), jnp.float32).at[:, :, center].add(message)  476 us
    gather x4, local copies, waits for them, and re-layouts, site_energies(): beside_all = gamma[:, :, center]  92.9 us
    gather x4, local copies, waits for them, and re-layouts, site_energies(): jnp.zeros((9, chans, atoms), jnp.float32).at[:, :, center].add(message)  92.8 us
    add_any x2, local copies, waits for them, and re-layouts, site_energies(): scalar0 = tensor[0] * beside_all[0]  37.1 us
    scatter-add x2, other arithmetic, site_energies(): delta = all_pos[:, neighbour] - all_pos[:, center]  36.9 us
    mul x2, local copies, waits for them, and re-layouts, site_energies(): message = embed[None] * harmonic[:, None]  36.8 us
    dot_general x16, matrix products, matmul(): return jnp.dot(weight.T, data, precision=lax.Precision.HIGHEST)  31.9 us
  transfers between devices with their start and end apart: 12, of which 5 were waited for; matrix products, arithmetic and copies ran while one was open for 3% of the time, Pallas kernels for 0%

commit v1 on v0

v1 whole, which is shorter than its diff:
```python
import functools

import jax
import jax.numpy as jnp
from jax import lax
from jax.experimental import pallas as pl
from jax.experimental.pallas import tpu as pltpu
from jax.sharding import PartitionSpec as P

edge_length = 3.0
env_scale = 0.125
root_three = 1.7320508075688772
axes = ("gx", "gy", "gz")
MESH = pl.DeviceIdType.MESH
f32 = jnp.float32
bf16 = jnp.bfloat16
C = 64
SLOTS = [k for k in range(27) if k != 13]
ROWS = 72
TILE = 256


def offset(k):
    return (k // 9 - 1, k // 3 % 3 - 1, k % 3 - 1)


def peer(k, sign):
    me = [lax.axis_index(a) for a in axes]
    sizes = [lax.axis_size(a) for a in axes]
    return tuple(lax.rem(m + sign * o + s, s) for m, o, s in zip(me, offset(k), sizes))


def greet():
    barrier = pltpu.get_barrier_semaphore()
    for k in SLOTS:
        pl.semaphore_signal(barrier, inc=1, device_id=peer(k, 1), device_id_type=MESH)
    pl.semaphore_wait(barrier, len(SLOTS))


def dot(a, b):
    return jnp.dot(a, b, preferred_element_type=f32)


def dot_nt(a, b):
    return lax.dot_general(a, b, (((1,), (1,)), ((), ())), preferred_element_type=f32)


def hi(x):
    return x.astype(bf16).astype(f32)


def halves(x):
    first = x.astype(bf16)
    return first, (x - first.astype(f32)).astype(bf16)


def thirds(x):
    first = hi(x)
    rest = x - first
    second = hi(rest)
    return first, second, rest - second


def halo_kernel(pos_ref, feat_ref, rows_ref, out_ref, send_buf, send_sem, recv_sem):
    greet()
    atoms = feat_ref.shape[1]
    sent = rows_ref.shape[1]
    pick = (
        lax.broadcasted_iota(jnp.int32, (atoms, sent), 0)
        == jnp.broadcast_to(rows_ref[...], (atoms, sent))
    ).astype(bf16)
    send_buf[0:C, :] = dot(feat_ref[...], pick)
    parts = thirds(pos_ref[...])
    send_buf[C : C + 3, :] = (
        dot(parts[0].astype(bf16), pick)
        + dot(parts[1].astype(bf16), pick)
        + dot(parts[2].astype(bf16), pick)
    )
    send_buf[C + 3 : ROWS, :] = jnp.zeros((ROWS - C - 3, sent), f32)
    copies = []
    for k in SLOTS:
        copy = pltpu.make_async_remote_copy(
            src_ref=send_buf,
            dst_ref=out_ref.at[k],
            send_sem=send_sem.at[k],
            recv_sem=recv_sem.at[k],
            device_id=peer(k, -1),
            device_id_type=MESH,
        )
        copy.start()
        copies.append(copy)
    out_ref[13] = jnp.zeros((ROWS, sent), f32)
    for copy in copies:
        copy.wait()


def halo(positions, features, rows):
    sent = rows.shape[1]
    return pl.pallas_call(
        halo_kernel,
        out_shape=jax.ShapeDtypeStruct((27, ROWS, sent), f32),
        in_specs=[pl.BlockSpec(memory_space=pltpu.VMEM)] * 3,
        out_specs=pl.BlockSpec(memory_space=pltpu.VMEM),
        scratch_shapes=[
            pltpu.VMEM((ROWS, sent), f32),
            pltpu.SemaphoreType.DMA((27,)),
            pltpu.SemaphoreType.DMA((27,)),
        ],
        compiler_params=pltpu.CompilerParams(collective_id=0, has_side_effects=True),
    )(positions, features, rows)


def return_kernel(ghost_ref, own_ref, rows_ref, force_ref, landed, send_sem, recv_sem):
    greet()
    copies = []
    for k in SLOTS:
        copy = pltpu.make_async_remote_copy(
            src_ref=ghost_ref.at[k],
            dst_ref=landed.at[k],
            send_sem=send_sem.at[k],
            recv_sem=recv_sem.at[k],
            device_id=peer(k, 1),
            device_id_type=MESH,
        )
        copy.start()
        copies.append(copy)
    atoms = own_ref.shape[1]
    sent = rows_ref.shape[1]
    pick = (
        lax.broadcasted_iota(jnp.int32, (atoms, sent), 0)
        == jnp.broadcast_to(rows_ref[...], (atoms, sent))
    ).astype(bf16)
    for copy in copies:
        copy.wait()
    owned = landed[SLOTS[0]]
    for k in SLOTS[1:]:
        owned = owned + landed[k]
    parts = thirds(owned)
    back = (
        dot_nt(parts[0].astype(bf16), pick)
        + dot_nt(parts[1].astype(bf16), pick)
        + dot_nt(parts[2].astype(bf16), pick)
    )
    force_ref[...] = -(own_ref[...] + back[0:3, :])


def give_back(ghost_grad, own_grad, rows):
    sent = rows.shape[1]
    return pl.pallas_call(
        return_kernel,
        out_shape=jax.ShapeDtypeStruct(own_grad.shape, f32),
        in_specs=[pl.BlockSpec(memory_space=pltpu.VMEM)] * 3,
        out_specs=pl.BlockSpec(memory_space=pltpu.VMEM),
        scratch_shapes=[
            pltpu.VMEM((27, 8, sent), f32),
            pltpu.SemaphoreType.DMA((27,)),
            pltpu.SemaphoreType.DMA((27,)),
        ],
        compiler_params=pltpu.CompilerParams(collective_id=1, has_side_effects=True),
    )(ghost_grad, own_grad, rows)


def forward_stack(weight):
    first = hi(weight)
    return jnp.concatenate([first, first, weight - first], 0).T.astype(bf16)


def backward_stack(weight):
    first = hi(weight)
    return jnp.concatenate([first, first, weight - first], 1).astype(bf16)


def stacked(x):
    first, second = halves(x)
    return jnp.concatenate([first, second, first], 0)


def sigmoid(x):
    return 0.5 * jnp.tanh(0.5 * x) + 0.5


def fold(x):
    total = x[0:8]
    for i in range(1, C // 8):
        total = total + x[8 * i : 8 * i + 8]
    return total


def chan(m):
    return slice(m * C, (m + 1) * C)


def pair_kernel(
    table_ref, pos_ref, feat_ref, center_ref, nbr_ref, count_ref,
    emb_ref, value_ref, env_ref, path_ref, latent_ref, gate_ref, final_ref, out_ref,
    site_ref, own_ref, ghost_ref,
    w_emb, w_ve, w_ge, w_fin, w_finb, w_lat, w_latb, w_b1, w_b0, w_embb, w_path, w_out,
    tab_feat, tab_pos, tab_pos3, tab_own,
    hot, hot_t, near, slot_s, geo, harm, basis_s,
    x_s, xh_s, xl_s, d0_s, d1_s, v_s, g_s, e0_s, e1_s, t1_s, t2_s,
    dx_s, dv_s, dg_s, dg0_s, dt1_s, dt2_s, k1_s, k2_s, j1_s, j2_s, dy_s, eps_s,
    big_g, big_h, work, msg_h, msg_l, acc, cat, acc_own, acc_near,
):
    pairs = center_ref.shape[1]
    atoms = pos_ref.shape[1]
    T = TILE
    steps = pairs // T

    emb = emb_ref[...]
    emb_h = hi(emb)
    emb_l = emb - emb_h
    w_emb[...] = jnp.concatenate(
        [
            jnp.concatenate([emb_h, emb_h[2 * C :]], 0),
            jnp.concatenate([emb_l, jnp.zeros((8, C), f32)], 0),
        ],
        1,
    ).T.astype(bf16)
    w_embb[...] = backward_stack(emb[2 * C :])
    w_ve[...] = forward_stack(jnp.concatenate([value_ref[...], env_ref[0]], 1))
    w_ge[...] = forward_stack(jnp.concatenate([gate_ref[0], env_ref[1]], 1))
    w_b0[...] = backward_stack(jnp.concatenate([env_ref[0], value_ref[...]], 1))
    w_b1[...] = backward_stack(jnp.concatenate([env_ref[1], gate_ref[0]], 1))
    w_fin[...] = forward_stack(final_ref[...])
    w_finb[...] = backward_stack(final_ref[...])
    w_out[...] = jnp.broadcast_to(out_ref[...], (8, C)).T
    for layer in range(2):
        cols = jnp.concatenate([path_ref[layer], jnp.ones((1, C), f32)], 0).T
        if layer == 0:
            w_path[...] = cols
        scaled = jnp.concatenate(
            [latent_ref[layer, 0:C]]
            + [latent_ref[layer, chan(i + 1)] * cols[:, i : i + 1] for i in range(3)],
            0,
        )
        first = hi(scaled)
        w_lat[layer] = jnp.concatenate([first, scaled - first], 1).T.astype(bf16)
        w_latb[layer] = backward_stack(scaled)

    tab_pos[...] = jnp.zeros(tab_pos.shape, f32)
    tab_feat[0:C, :] = feat_ref[:, 0:128]
    tab_feat[C : 2 * C, :] = feat_ref[:, 128:256]
    for k in range(27):
        tab_feat[(k + 2) * C : (k + 3) * C, :] = table_ref[k, 0:C, :].astype(bf16)
    for c in range(3):
        tab_pos[c * 32 : c * 32 + 1, :] = pos_ref[c : c + 1, 0:128]
        tab_pos[c * 32 + 1 : c * 32 + 2, :] = pos_ref[c : c + 1, 128:256]
        for k in range(27):
            tab_pos[c * 32 + k + 2 : c * 32 + k + 3, :] = (
                table_ref[k, C + c : C + c + 1, :] + edge_length * offset(k)[c]
            )
    for i, part in enumerate(thirds(tab_pos[...])):
        tab_pos3[i * 96 : (i + 1) * 96, :] = part.astype(bf16)
    tab_own[0:C, :] = feat_ref[...]
    tab_own[C : C + 16, :] = jnp.concatenate(
        list(thirds(pos_ref[...])) + [jnp.zeros((7, atoms), f32)], 0
    ).astype(bf16)

    def span(t):
        return pl.ds(pl.multiple_of(t * T, T), T)

    def live_at(t):
        at = lax.broadcasted_iota(jnp.int32, (1, T), 1) + t * T
        return jnp.where(at < jnp.broadcast_to(count_ref[...], (1, T)), 1.0, 0.0)

    def scatter(t):
        return dot(msg_h[...], hot[span(t), :]) + dot(msg_l[...], hot[span(t), :])

    def put(m, x):
        first, second = halves(x)
        msg_h[chan(m), :] = first
        msg_l[chan(m), :] = second

    def make_cat():
        first, second = halves(acc[...])
        cat[:, 0:atoms] = first
        cat[:, atoms : 2 * atoms] = second

    def latent(layer, xh, xl, scalars):
        split = [halves(s) for s in scalars]
        high = jnp.concatenate([xh] + [s[0] for s in split], 0)
        low = jnp.concatenate([xl] + [s[1] for s in split], 0)
        both = dot(w_lat[layer], high)
        return both[0:C] + both[C:] + dot(w_lat[layer, 0:C], low)

    def phase_a(t, carry):
        at = span(t)
        nbr = nbr_ref[:, at]
        rest = jnp.bitwise_and(nbr, 127)
        slot = jnp.right_shift(nbr, 7)
        r = (
            lax.broadcasted_iota(jnp.int32, (128, T), 0) == jnp.broadcast_to(rest, (128, T))
        ).astype(bf16)
        near[:, at] = r
        s = jnp.where(
            lax.broadcasted_iota(jnp.int32, (32, T), 0) == jnp.broadcast_to(slot, (32, T)), 1.0, 0.0
        )
        slot_s[:, at] = s
        own = (
            lax.broadcasted_iota(jnp.int32, (atoms, T), 0)
            == jnp.broadcast_to(center_ref[:, at], (atoms, T))
        ).astype(f32)
        hot_t[0:atoms, at] = own.astype(bf16)
        hot_t[atoms : 2 * atoms, at] = own.astype(bf16)
        hot[at, :] = own.T.astype(bf16)
        found = dot(tab_own[...], hot_t[0:atoms, at])
        feat_i = found[0:C]
        pos_i = found[C : C + 3] + found[C + 3 : C + 6] + found[C + 6 : C + 9]
        far = dot(tab_pos3[...], r)
        far = far[0:96] + far[96:192] + far[192:288]
        pos_j = jnp.concatenate(
            [jnp.sum(far[c * 32 : c * 32 + 32] * s, 0, keepdims=True) for c in range(3)], 0
        )
        feat_j = jnp.zeros((C, T), f32)
        for k0 in range(0, 29, 8):
            many = min(8, 29 - k0)
            got = dot(tab_feat[k0 * C : (k0 + many) * C, :], r)
            for k in range(many):
                feat_j = feat_j + got[chan(k)] * s[k0 + k : k0 + k + 1]
        d = pos_j - pos_i
        rho = jnp.sqrt(jnp.sum(d * d, 0, keepdims=True) + 1.0)
        inv = 1.0 / rho
        u = d * inv
        ux, uy, uz = u[0:1], u[1:2], u[2:3]
        y = [
            None, ux, uy, uz,
            root_three * ux * uy,
            root_three * uy * uz,
            root_three * uz * ux,
            (root_three * 0.5) * (ux * ux - uy * uy),
            0.5 * (2.0 * uz * uz - ux * ux - uy * uy),
        ]
        for m in range(1, 9):
            harm[m : m + 1, at] = y[m]
        geo[0:3, at] = u
        geo[3:4, at] = rho
        mu = lax.broadcasted_iota(jnp.int32, (8, T), 0).astype(f32) * 1.25
        z = rho - mu
        basis = jnp.exp(-0.5 * z * z)
        basis_s[:, at] = basis * z
        joined = jnp.concatenate(
            [
                feat_i.astype(bf16),
                feat_j.astype(bf16),
                jnp.concatenate([basis, basis - hi(basis)], 0).astype(bf16),
            ],
            0,
        )
        pre = dot(w_emb[...], joined)
        pre = pre[0:C] + pre[C:]
        sg = sigmoid(pre)
        x = pre * sg
        d0_s[:, at] = sg * (1.0 + pre * (1.0 - sg))
        xh, xl = halves(x)
        x_s[:, at] = x
        xh_s[:, at] = xh
        xl_s[:, at] = xl
        ve = dot(w_ve[...], jnp.concatenate([xh, xl, xh], 0))
        v_s[:, at] = ve[0:C]
        e = ve[C:] * (env_scale * live_at(t))
        e0_s[:, at] = e
        put(0, e)
        for m in range(1, 9):
            put(m, e * y[m])
        acc[...] += scatter(t)
        return carry

    def phase_b(t, carry):
        at = span(t)
        big_g[:, at] = dot(cat[...], hot_t[:, at])
        g0 = big_g[chan(0), at]
        t1 = big_g[chan(1), at] * harm[1:2, at]
        for m in range(2, 4):
            t1 = t1 + big_g[chan(m), at] * harm[m : m + 1, at]
        t2 = big_g[chan(4), at] * harm[4:5, at]
        for m in range(5, 9):
            t2 = t2 + big_g[chan(m), at] * harm[m : m + 1, at]
        t1_s[:, at] = t1
        t2_s[:, at] = t2
        v = v_s[:, at]
        pre = latent(0, xh_s[:, at], xl_s[:, at], [v * g0, v * t1, v * t2])
        sg = sigmoid(pre)
        x = x_s[:, at] + pre * sg
        d1_s[:, at] = sg * (1.0 + pre * (1.0 - sg))
        xh, xl = halves(x)
        x_s[:, at] = x
        xh_s[:, at] = xh
        xl_s[:, at] = xl
        ge = dot(w_ge[...], jnp.concatenate([xh, xl, xh], 0))
        g_s[:, at] = ge[0:C]
        e = ge[C:] * (env_scale * live_at(t))
        e1_s[:, at] = e
        put(0, e)
        for m in range(1, 9):
            put(m, e * harm[m : m + 1, at])
        acc[...] += scatter(t)
        return carry

    def path(i):
        return w_path[:, i : i + 1]

    def phase_c(t, carry):
        at = span(t)
        big_h[:, at] = dot(cat[...], hot_t[:, at])

        def sums(low, high):
            a = big_g[chan(low), at] * big_h[chan(low), at]
            b = big_h[chan(low), at] * harm[low : low + 1, at]
            for m in range(low + 1, high):
                h = big_h[chan(m), at]
                a = a + big_g[chan(m), at] * h
                b = b + h * harm[m : m + 1, at]
            return a, b

        a1, b1 = sums(1, 4)
        a2, b2 = sums(4, 9)
        g0 = big_g[chan(0), at]
        h0 = big_h[chan(0), at]
        c0 = path(0) * g0 + path(1) * t1_s[:, at] + path(2) * t2_s[:, at]
        h4 = path(4) * g0
        h6 = path(6) * g0
        p0 = c0 * h0
        p1 = path(3) * a1 + h4 * b1
        p2 = path(5) * a2 + h6 * b2
        v = v_s[:, at]
        g = g_s[:, at]
        gv = g * v
        pre = latent(1, xh_s[:, at], xl_s[:, at], [gv * p0, gv * p1, gv * p2])
        sg = sigmoid(pre)
        x = x_s[:, at] + pre * sg
        d2 = sg * (1.0 + pre * (1.0 - sg))
        hid = dot(w_fin[...], stacked(x))
        sg = sigmoid(hid)
        live = live_at(t)
        ow = w_out[:, 0:1]
        eps_s[:, at] = jnp.sum(fold(ow * (hid * sg)), 0, keepdims=True) * live
        dhid = (ow * live) * (sg * (1.0 + hid * (1.0 - sg)))
        dx = dot(w_finb[...], stacked(dhid))
        dm = dot(w_latb[1], stacked(dx * d2))
        dx_s[:, at] = dx + dm[0:C]
        ds0, ds1, ds2 = dm[chan(1)], dm[chan(2)], dm[chan(3)]
        dgv = ds0 * p0 + ds1 * p1 + ds2 * p2
        dg_s[:, at] = dgv * v
        dv_s[:, at] = dgv * g
        u0 = ds0 * gv
        u1 = ds1 * gv
        u2 = ds2 * gv
        k1 = u1 * path(3)
        k2 = u2 * path(5)
        j1 = u1 * h4
        j2 = u2 * h6
        k1_s[:, at] = k1
        k2_s[:, at] = k2
        j1_s[:, at] = j1
        j2_s[:, at] = j2
        uh = u0 * h0
        dg0_s[:, at] = uh * path(0) + u1 * path(4) * b1 + u2 * path(6) * b2
        dt1_s[:, at] = uh * path(1)
        dt2_s[:, at] = uh * path(2)
        put(0, u0 * c0)
        for m in range(1, 9):
            k, j = (k1, j1) if m < 4 else (k2, j2)
            put(m, k * big_g[chan(m), at] + j * harm[m : m + 1, at])
        acc[...] += scatter(t)
        return carry

    def phase_d(t, carry):
        at = span(t)
        work[...] = dot(cat[...], hot_t[:, at])
        de = work[chan(0), :]
        for m in range(1, 9):
            de = de + work[chan(m), :] * harm[m : m + 1, at]
        de = de * (env_scale * live_at(t))
        deh, del_ = halves(de)
        dgh, dgl = halves(dg_s[:, at])
        dx = dx_s[:, at] + dot(
            w_b1[...], jnp.concatenate([deh, dgh, del_, dgl, deh, dgh], 0)
        )
        dm = dot(w_latb[0], stacked(dx * d1_s[:, at]))
        dx_s[:, at] = dx + dm[0:C]
        ds0, ds1, ds2 = dm[chan(1)], dm[chan(2)], dm[chan(3)]
        v = v_s[:, at]
        dv_s[:, at] += ds0 * big_g[chan(0), at] + ds1 * t1_s[:, at] + ds2 * t2_s[:, at]
        dt1 = dt1_s[:, at] + ds1 * v
        dt2 = dt2_s[:, at] + ds2 * v
        put(0, dg0_s[:, at] + ds0 * v)
        e = e1_s[:, at]
        for m in range(1, 9):
            if m < 4:
                k, j, dt = k1_s[:, at], j1_s[:, at], dt1
            else:
                k, j, dt = k2_s[:, at], j2_s[:, at], dt2
            h = big_h[chan(m), at]
            dy_s[8 * m : 8 * m + 8, at] = fold(
                j * h + dt * big_g[chan(m), at] + e * work[chan(m), :]
            )
            put(m, k * h + dt * harm[m : m + 1, at])
        acc[...] += scatter(t)
        return carry

    def phase_e(t, carry):
        at = span(t)
        work[...] = dot(cat[...], hot_t[:, at])
        de = work[chan(0), :]
        for m in range(1, 9):
            de = de + work[chan(m), :] * harm[m : m + 1, at]
        de = de * (env_scale * live_at(t))
        e = e0_s[:, at]
        dy = [None]
        for m in range(1, 9):
            part = dy_s[8 * m : 8 * m + 8, at] + fold(e * work[chan(m), :])
            dy.append(jnp.sum(part, 0, keepdims=True))
        deh, del_ = halves(de)
        dvh, dvl = halves(dv_s[:, at])
        dx = dx_s[:, at] + dot(
            w_b0[...], jnp.concatenate([deh, dvh, del_, dvl, deh, dvh], 0)
        )
        dbasis = dot(w_embb[...], stacked(dx * d0_s[:, at]))
        drho = -jnp.sum(dbasis * basis_s[:, at], 0, keepdims=True)
        u = geo[0:3, at]
        rho = geo[3:4, at]
        inv = 1.0 / rho
        ux, uy, uz = u[0:1], u[1:2], u[2:3]
        dux = dy[1] + root_three * (uy * dy[4] + uz * dy[6] + ux * dy[7]) - ux * dy[8]
        duy = dy[2] + root_three * (ux * dy[4] + uz * dy[5] - uy * dy[7]) - uy * dy[8]
        duz = dy[3] + root_three * (uy * dy[5] + ux * dy[6]) + 2.0 * (uz * dy[8])
        along = drho - (dux * ux + duy * uy + duz * uz) * inv
        dd = [dux * inv + ux * along, duy * inv + uy * along, duz * inv + uz * along]
        rows = jnp.concatenate(dd + [eps_s[:, at]], 0)
        first = hi(rows)
        rest = rows - first
        second = hi(rest)
        acc_own[...] += dot(
            jnp.concatenate([first, second, rest - second, jnp.zeros((4, T), f32)], 0).astype(bf16),
            hot[at, :],
        )
        s = slot_s[:, at]
        spread = jnp.concatenate([s * dd[c] for c in range(3)], 0)
        first = hi(spread)
        acc_near[...] += dot_nt(
            jnp.concatenate([first, spread - first], 0).astype(bf16), near[:, at]
        )
        return carry

    acc[...] = jnp.zeros(acc.shape, f32)
    lax.fori_loop(0, steps, phase_a, 0)
    for phase in (phase_b, phase_c, phase_d):
        make_cat()
        acc[...] = jnp.zeros(acc.shape, f32)
        lax.fori_loop(0, steps, phase, 0)
    make_cat()
    acc_own[...] = jnp.zeros(acc_own.shape, f32)
    acc_near[...] = jnp.zeros(acc_near.shape, f32)
    lax.fori_loop(0, steps, phase_e, 0)

    own = acc_own[0:4, :] + acc_own[4:8, :] + acc_own[8:12, :]
    site_ref[...] = own[3:4, :]
    ghosts = acc_near[0:96, :] + acc_near[96:192, :]
    for c in range(3):
        local = jnp.concatenate([ghosts[c * 32 : c * 32 + 1], ghosts[c * 32 + 1 : c * 32 + 2]], 1)
        own_ref[c : c + 1, :] = local - own[c : c + 1]
    ghost_ref[...] = jnp.zeros(ghost_ref.shape, f32)
    for k in range(27):
        for c in range(3):
            ghost_ref[k, c : c + 1, :] = ghosts[c * 32 + k + 2 : c * 32 + k + 3, :]


def pair_grads(table, positions, features, center, nbr, count, params):
    pairs = center.shape[1]
    atoms = positions.shape[1]
    T = TILE

    def wide(rows, dtype=f32):
        return pltpu.VMEM((rows, pairs), dtype)

    scratch = [
        pltpu.VMEM((128, 144), bf16),
        pltpu.VMEM((128, 192), bf16),
        pltpu.VMEM((128, 192), bf16),
        pltpu.VMEM((64, 192), bf16),
        pltpu.VMEM((64, 192), bf16),
        pltpu.VMEM((2, 128, 256), bf16),
        pltpu.VMEM((2, 256, 192), bf16),
        pltpu.VMEM((64, 384), bf16),
        pltpu.VMEM((64, 384), bf16),
        pltpu.VMEM((8, 192), bf16),
        pltpu.VMEM((64, 8), f32),
        pltpu.VMEM((64, 8), f32),
        pltpu.VMEM((29 * 64, 128), bf16),
        pltpu.VMEM((96, 128), f32),
        pltpu.VMEM((288, 128), bf16),
        pltpu.VMEM((80, atoms), bf16),
        pltpu.VMEM((pairs, atoms), bf16),
        wide(2 * atoms, bf16),
        wide(128, bf16),
        wide(32),
        wide(8),
        wide(16),
        wide(8),
        wide(64),
        wide(64, bf16),
        wide(64, bf16),
    ]
    scratch += [wide(64)] * 18
    scratch[-1] = wide(64)
    scratch += [wide(72), wide(1)]
    scratch += [
        wide(576),
        wide(576),
        pltpu.VMEM((576, T), f32),
        pltpu.VMEM((576, T), bf16),
        pltpu.VMEM((576, T), bf16),
        pltpu.VMEM((576, atoms), f32),
        pltpu.VMEM((576, 2 * atoms), bf16),
        pltpu.VMEM((16, atoms), f32),
        pltpu.VMEM((192, 128), f32),
    ]
    vmem = pl.BlockSpec(memory_space=pltpu.VMEM)
    return pl.pallas_call(
        pair_kernel,
        out_shape=(
            jax.ShapeDtypeStruct((1, atoms), f32),
            jax.ShapeDtypeStruct((3, atoms), f32),
            jax.ShapeDtypeStruct((27, 8, 128), f32),
        ),
        in_specs=[vmem] * 14,
        out_specs=(vmem, vmem, vmem),
        scratch_shapes=scratch,
        compiler_params=pltpu.CompilerParams(vmem_limit_bytes=60 * 1024 * 1024),
        cost_estimate=pl.CostEstimate(flops=40 * 10**9, bytes_accessed=10**6, transcendentals=10**6),
    )(table, positions, features, center, nbr, count, *params)


def local(
    positions, features, ghost_rows, pair_center, pair_nbr, pair_count,
    emb_weight, value_weight, env_weight, path_weight, latent_weight, gate_weight,
    final_weight, out_weight,
):
    rows = ghost_rows.reshape(1, -1)
    table = halo(positions, features, rows)
    site, own, ghost = pair_grads(
        table, positions, features,
        pair_center.reshape(1, -1), pair_nbr.reshape(1, -1), pair_count.reshape(1, 1),
        (emb_weight, value_weight, env_weight, path_weight, latent_weight, gate_weight,
         final_weight, out_weight.reshape(1, -1)),
    )
    forces = give_back(ghost, own, rows)
    return (site.reshape(-1), forces)


def solution(mesh):
    placed = (
        P(None, axes),
        P(None, axes),
        P(axes),
        P(axes),
        P(axes),
        P(axes),
    ) + (P(),) * 8
    return jax.shard_map(
        local,
        mesh=mesh,
        in_specs=placed,
        out_specs=(P(axes), P(None, axes)),
        check_vma=False,
    )
```

time: 1570 us -> 120 us (0.08); the launches traced: 1550 us -> 119 us
  other arithmetic: 1120 us -> 0 us
  local copies, waits for them, and re-layouts: 350 us -> 4.98 us
  Pallas kernels: 0 us -> 113 us
  matrix products: 33.8 us -> 0 us
  starting transfers between devices: 23 us -> 0 us
    scatter-add x8 -> x0, other arithmetic: 1010 us -> none  [the longest x2 476 us: site_energies(): beside_all = gamma[:, :, center]]
    gather x17 -> x0, local copies, waits for them, and re-layouts: 255 us -> none  [the longest x4 92.9 us: site_energies(): beside_all = gamma[:, :, center]]
    pallas_call x0 -> x3, Pallas kernels: none -> 113 us  [the longest x1 80.1 us: pair_grads(): pl.pallas_call(pair_kernel, out_shape=(jax.ShapeDtypeStruct((1, atoms), f...]
    mul x25 -> x0, other arithmetic: 39 us -> none  [the longest x2 10.1 us: site_energies(): tensor = jnp.concatenate([part0, part1, part2], 0) * gating[None]]
    mul x4 -> x0, local copies, waits for them, and re-layouts: 38.9 us -> none  [the longest x2 36.8 us: site_energies(): message = embed[None] * harmonic[:, None]]
    add_any x3 -> x0, local copies, waits for them, and re-layouts: 37.6 us -> none  [the longest x2 37.1 us: site_energies(): scalar0 = tensor[0] * beside_all[0]]
    dot_general x17 -> x0, matrix products: 33.8 us -> none  [the longest x16 31.9 us: matmul(): return jnp.dot(weight.T, data, precision=lax.Precision.HIGHEST)]
    reduce_sum x10 -> x0, other arithmetic: 32.4 us -> none  [the longest x1 8.82 us: site_energies(): weights[4] * tensor[1:4] * beside_all[0][None]]
  transfers between devices with their start and end apart: 12 -> 0, of which waited for: 5 -> 0; matrix products, arithmetic and copies ran while one was open for 3% -> 0% of each run, Pallas kernels for 0% -> 0%
where the time goes in v1:
time: 120 us; the launch traced here: 119 us
  Pallas kernels  113 us (94%)
  local copies, waits for them, and re-layouts  4.98 us (4%)
  between operations  1.34 us (1%)
    pallas_call x1, Pallas kernels, pair_grads(): pl.pallas_call(pair_kernel, out_shape=(jax.ShapeDtypeStruct((1, atoms), f...  80.1 us
    pallas_call x1, Pallas kernels, halo(): pl.pallas_call(halo_kernel, out_shape=jax.ShapeDtypeStruct((27, ROWS, sen...  21.2 us
    pallas_call x1, Pallas kernels, give_back(): pl.pallas_call(return_kernel, out_shape=jax.ShapeDtypeStruct(own_grad.sha...  11.6 us
    unnamed x6, local copies, waits for them, and re-layouts  4.98 us

profile of v1, /device:TPU:1, one launch (start us, length us, event | category | flops | bytes accessed | tf_op | source)
XLA Modules:
  0.0 119.2 jit_solution(15335257439743699072)
XLA Ops:
  0.6 0.0 copy-start
  1.3 1.3 %copy.17.path_ref = f32[2,7,64]{2,1,0:T(8,128)} copy(f32[2,7,64]{2,0,1:T(2,128)} %param.23) | data formatting | bytes 7168 | tf_op args[9]
  2.6 1.6 %copy.16.emb_ref = f32[136,64]{1,0:T(8,128)} copy(f32[136,64]{0,1:T(8,128)} %param.20) | data formatting | bytes 69632 | tf_op args[6]
  4.2 0.0 copy-done
  4.2 0.9 copy.18.latent_ref
  5.0 21.2 %shard_map.149.table_ref = f32[27,72,128]{2,1,0:T(8,128)} custom-call(f32[3,256]{1,0:T(4,128)} %pos_ref.3, bf16[64,256]{1,0:T(8,128)(2,1)} %feat_ref.3, s32[1,128]{1,0:T(1,128)} %bitcast.7), custom_call_target="tpu_custom_call" | custom-call | tf_op jit(solution)/shard_map/pallas_call | solution.py:99
  26.3 80.1 %shard_map.150 = (f32[1,256]{1,0:T(1,128)}, f32[3,256]{1,0:T(4,128)}, f32[27,8,128]{2,1,0:T(8,128)}) custom-call(f32[27,72,128]{2,1,0:T(8,128)} %shard_map.149.table_ref, f32[3,256]{1,0:T(4,128)} %pos_ref.3, bf16[64,256]{1,0:T(8,128)(2,1)} %feat_ref.3, s32[1,3072]{1,0:T(1,128)} %bitcast.9, s32[1,3072]{1,0:T(1,128)} %bitcast.10, s32[1,1]{1,0:T(1,128)} %bitcast.6.count_ref, ...), custom_call_target="tpu_custom_call" | custom-call | flops 40000000000 | bytes 1000000 | tf_op jit(solution)/shard_map/pallas_call | solution.py:619
  106.4 11.6 %shard_map.151 = f32[3,256]{1,0:T(4,128)} custom-call(f32[27,8,128]{2,1,0:T(8,128)} %get-tuple-element.6.ghost_ref, f32[3,256]{1,0:T(4,128)} %get-tuple-element.7.own_ref, s32[1,128]{1,0:T(1,128)} %bitcast.8), custom_call_target="tpu_custom_call" | custom-call | tf_op jit(solution)/shard_map/pallas_call | solution.py:149
  117.9 1.3 %copy.21 = f32[3,256]{1,0:T(4,128)} copy(f32[3,256]{1,0:T(4,128)} %shard_map.151) | data formatting | bytes 6144
Async XLA Ops:
  0.6 3.6 %copy-start = (f32[2,256,64]{1,2,0:T(8,128)S(1)}, f32[2,256,64]{1,2,0:T(8,128)}, u32[]{:S(2)}) copy-start(f32[2,256,64]{1,2,0:T(8,128)} %param.24) | copy-start | bytes 393220

commit v2 on v1

--- a/solution.py
+++ b/solution.py
@@ -18,6 +18,9 @@
 SLOTS = [k for k in range(27) if k != 13]
 ROWS = 72
 TILE = 256
+SKEW = 1
+GROUP = 3
+RING = 6
 
 
 def offset(k):
@@ -206,94 +209,138 @@
     T = TILE
     steps = pairs // T
 
-    emb = emb_ref[...]
-    emb_h = hi(emb)
-    emb_l = emb - emb_h
-    w_emb[...] = jnp.concatenate(
-        [
-            jnp.concatenate([emb_h, emb_h[2 * C :]], 0),
-            jnp.concatenate([emb_l, jnp.zeros((8, C), f32)], 0),
-        ],
-        1,
-    ).T.astype(bf16)
-    w_embb[...] = backward_stack(emb[2 * C :])
-    w_ve[...] = forward_stack(jnp.concatenate([value_ref[...], env_ref[0]], 1))
-    w_ge[...] = forward_stack(jnp.concatenate([gate_ref[0], env_ref[1]], 1))
-    w_b0[...] = backward_stack(jnp.concatenate([env_ref[0], value_ref[...]], 1))
-    w_b1[...] = backward_stack(jnp.concatenate([env_ref[1], gate_ref[0]], 1))
-    w_fin[...] = forward_stack(final_ref[...])
-    w_finb[...] = backward_stack(final_ref[...])
-    w_out[...] = jnp.broadcast_to(out_ref[...], (8, C)).T
-    for layer in range(2):
-        cols = jnp.concatenate([path_ref[layer], jnp.ones((1, C), f32)], 0).T
-        if layer == 0:
-            w_path[...] = cols
-        scaled = jnp.concatenate(
-            [latent_ref[layer, 0:C]]
-            + [latent_ref[layer, chan(i + 1)] * cols[:, i : i + 1] for i in range(3)],
+    stage = pl.program_id(0)
+
+    @pl.when(stage == 0)
+    def _():
+        emb = emb_ref[...]
+        emb_h = hi(emb)
+        emb_l = emb - emb_h
+        w_emb[...] = jnp.concatenate(
+            [
+                jnp.concatenate([emb_h, emb_h[2 * C :]], 0),
+                jnp.concatenate([emb_l, jnp.zeros((8, C), f32)], 0),
+            ],
+            1,
+        ).T.astype(bf16)
+        low_h = emb_h[2 * C :]
+        w_embb[...] = jnp.concatenate(
+            [
+                jnp.concatenate([low_h, low_h], 1),
+                jnp.concatenate([emb_l[2 * C :], jnp.zeros((8, C), f32)], 1),
+            ],
             0,
-        )
-        first = hi(scaled)
-        w_lat[layer] = jnp.concatenate([first, scaled - first], 1).T.astype(bf16)
-        w_latb[layer] = backward_stack(scaled)
-
-    tab_pos[...] = jnp.zeros(tab_pos.shape, f32)
-    tab_feat[0:C, :] = feat_ref[:, 0:128]
-    tab_feat[C : 2 * C, :] = feat_ref[:, 128:256]
-    for k in range(27):
-        tab_feat[(k + 2) * C : (k + 3) * C, :] = table_ref[k, 0:C, :].astype(bf16)
-    for c in range(3):
-        tab_pos[c * 32 : c * 32 + 1, :] = pos_ref[c : c + 1, 0:128]
-        tab_pos[c * 32 + 1 : c * 32 + 2, :] = pos_ref[c : c + 1, 128:256]
+        ).astype(bf16)
+        w_ve[...] = forward_stack(jnp.concatenate([value_ref[...], env_ref[0]], 1))
+        w_ge[...] = forward_stack(jnp.concatenate([gate_ref[0], env_ref[1]], 1))
+        w_b0[...] = backward_stack(jnp.concatenate([env_ref[0], value_ref[...]], 1))
+        w_b1[...] = backward_stack(jnp.concatenate([env_ref[1], gate_ref[0]], 1))
+        w_fin[...] = forward_stack(final_ref[...])
+        w_finb[...] = backward_stack(final_ref[...])
+        w_out[...] = jnp.broadcast_to(out_ref[...], (8, C)).T
+        for layer in range(2):
+            cols = jnp.concatenate([path_ref[layer], jnp.ones((1, C), f32)], 0).T
+            if layer == 0:
+                w_path[...] = cols
+            scaled = jnp.concatenate(
+                [latent_ref[layer, 0:C]]
+                + [latent_ref[layer, chan(i + 1)] * cols[:, i : i + 1] for i in range(3)],
+                0,
+            )
+            first = hi(scaled)
+            w_lat[layer] = jnp.concatenate([first, scaled - first], 1).T.astype(bf16)
+            w_latb[layer] = backward_stack(scaled)
+
+        tab_pos[...] = jnp.zeros(tab_pos.shape, f32)
+        tab_feat[0:C, :] = feat_ref[...]
+        tab_feat[14 * C : 15 * C, 128:256] = jnp.zeros((C, 128), bf16)
         for k in range(27):
-            tab_pos[c * 32 + k + 2 : c * 32 + k + 3, :] = (
-                table_ref[k, C + c : C + c + 1, :] + edge_length * offset(k)[c]
-            )
-    for i, part in enumerate(thirds(tab_pos[...])):
-        tab_pos3[i * 96 : (i + 1) * 96, :] = part.astype(bf16)
-    tab_own[0:C, :] = feat_ref[...]
-    tab_own[C : C + 16, :] = jnp.concatenate(
-        list(thirds(pos_ref[...])) + [jnp.zeros((7, atoms), f32)], 0
-    ).astype(bf16)
+            half = slice(k % 2 * 128, k % 2 * 128 + 128)
+            at = 1 + k // 2
+            tab_feat[chan(at), half] = table_ref[k, 0:C, :].astype(bf16)
+            for c in range(3):
+                tab_pos[c * 16 + at : c * 16 + at + 1, half] = (
+                    table_ref[k, C + c : C + c + 1, :] + edge_length * offset(k)[c]
+                )
+        for c in range(3):
+            tab_pos[c * 16 : c * 16 + 1, :] = pos_ref[c : c + 1, :]
+        for i, part in enumerate(thirds(tab_pos[...])):
+            tab_pos3[i * 48 : (i + 1) * 48, :] = part.astype(bf16)
+        tab_own[0:C, :] = feat_ref[...]
+        tab_own[C : C + 16, :] = jnp.concatenate(
+            list(thirds(pos_ref[...])) + [jnp.zeros((7, atoms), f32)], 0
+        ).astype(bf16)
 
     def span(t):
-        return pl.ds(pl.multiple_of(t * T, T), T)
+        return slice(t * T, (t + 1) * T)
 
     def live_at(t):
         at = lax.broadcasted_iota(jnp.int32, (1, T), 1) + t * T
         return jnp.where(at < jnp.broadcast_to(count_ref[...], (1, T)), 1.0, 0.0)
 
     def scatter(t):
-        return dot(msg_h[...], hot[span(t), :]) + dot(msg_l[...], hot[span(t), :])
-
-    def put(m, x):
+        many = GROUP
+        if t % many == many - 1:
+            at = slice((t + 1 - many) * T, (t + 1) * T)
+            late = t % RING
+            held = slice((late + 1 - many) * T, (late + 1) * T)
+            add = dot(msg_h[:, held], hot[at, :]) + dot(msg_l[:, held], hot[at, :])
+            if t == many - 1:
+                acc[...] = add
+            else:
+                acc[...] += add
+
+    def gather(t):
+        return dot(cat[...], hot_t[:, span(t)])
+
+    def put(m, t, x):
         first, second = halves(x)
-        msg_h[chan(m), :] = first
-        msg_l[chan(m), :] = second
+        msg_h[chan(m), span(t % RING)] = first
+        msg_l[chan(m), span(t % RING)] = second
 
     def make_cat():
         first, second = halves(acc[...])
         cat[:, 0:atoms] = first
         cat[:, atoms : 2 * atoms] = second
 
-    def latent(layer, xh, xl, scalars):
+    def spread_latent(xh, xl, scalars):
         split = [halves(s) for s in scalars]
         high = jnp.concatenate([xh] + [s[0] for s in split], 0)
         low = jnp.concatenate([xl] + [s[1] for s in split], 0)
+        return high, low
+
+    def latent(layer, high, low):
         both = dot(w_lat[layer], high)
         return both[0:C] + both[C:] + dot(w_lat[layer, 0:C], low)
 
-    def phase_a(t, carry):
+    def run(phase):
+        gens = [phase(t) for t in range(steps)]
+        done = 0
+        tick = 0
+        alive = [True] * steps
+        while any(alive):
+            for t in range(steps):
+                if alive[t] and tick >= t * SKEW:
+                    try:
+                        next(gens[t])
+                    except StopIteration:
+                        alive[t] = False
+            tick += 1
+
+    def row(m, at):
+        return harm[m : m + 1, at]
+
+    def phase_a(t):
         at = span(t)
         nbr = nbr_ref[:, at]
-        rest = jnp.bitwise_and(nbr, 127)
-        slot = jnp.right_shift(nbr, 7)
+        rest = jnp.bitwise_and(nbr, 255)
+        slot = jnp.right_shift(nbr, 8)
         r = (
-            lax.broadcasted_iota(jnp.int32, (128, T), 0) == jnp.broadcast_to(rest, (128, T))
+            lax.broadcasted_iota(jnp.int32, (256, T), 0) == jnp.broadcast_to(rest, (256, T))
         ).astype(bf16)
         near[:, at] = r
         s = jnp.where(
-            lax.broadcasted_iota(jnp.int32, (32, T), 0) == jnp.broadcast_to(slot, (32, T)), 1.0, 0.0
+            lax.broadcasted_iota(jnp.int32, (16, T), 0) == jnp.broadcast_to(slot, (16, T)), 1.0, 0.0
         )
         slot_s[:, at] = s
         own = (
@@ -303,20 +350,22 @@
         hot_t[0:atoms, at] = own.astype(bf16)
         hot_t[atoms : 2 * atoms, at] = own.astype(bf16)
         hot[at, :] = own.T.astype(bf16)
+        yield
         found = dot(tab_own[...], hot_t[0:atoms, at])
-        feat_i = found[0:C]
+        far = dot(tab_pos3[...], near[:, at])
+        yield
         pos_i = found[C : C + 3] + found[C + 3 : C + 6] + found[C + 6 : C + 9]
-        far = dot(tab_pos3[...], r)
-        far = far[0:96] + far[96:192] + far[192:288]
+        far = far[0:48] + far[48:96] + far[96:144]
         pos_j = jnp.concatenate(
-            [jnp.sum(far[c * 32 : c * 32 + 32] * s, 0, keepdims=True) for c in range(3)], 0
+            [jnp.sum(far[c * 16 : c * 16 + 16] * s, 0, keepdims=True) for c in range(3)], 0
         )
+        feat_i = found[0:C].astype(bf16)
         feat_j = jnp.zeros((C, T), f32)
-        for k0 in range(0, 29, 8):
-            many = min(8, 29 - k0)
-            got = dot(tab_feat[k0 * C : (k0 + many) * C, :], r)
-            for k in range(many):
+        for k0 in range(0, 15, 5):
+            got = dot(tab_feat[k0 * C : (k0 + 5) * C, :], near[:, at])
+            for k in range(5):
                 feat_j = feat_j + got[chan(k)] * s[k0 + k : k0 + k + 1]
+        yield
         d = pos_j - pos_i
         rho = jnp.sqrt(jnp.sum(d * d, 0, keepdims=True) + 1.0)
         inv = 1.0 / rho
@@ -340,13 +389,15 @@
         basis_s[:, at] = basis * z
         joined = jnp.concatenate(
             [
-                feat_i.astype(bf16),
+                feat_i,
                 feat_j.astype(bf16),
                 jnp.concatenate([basis, basis - hi(basis)], 0).astype(bf16),
             ],
             0,
         )
+        yield
         pre = dot(w_emb[...], joined)
+        yield
         pre = pre[0:C] + pre[C:]
         sg = sigmoid(pre)
         x = pre * sg
@@ -355,30 +406,36 @@
         x_s[:, at] = x
         xh_s[:, at] = xh
         xl_s[:, at] = xl
+        yield
         ve = dot(w_ve[...], jnp.concatenate([xh, xl, xh], 0))
+        yield
         v_s[:, at] = ve[0:C]
         e = ve[C:] * (env_scale * live_at(t))
         e0_s[:, at] = e
-        put(0, e)
+        put(0, t, e)
         for m in range(1, 9):
-            put(m, e * y[m])
-        acc[...] += scatter(t)
-        return carry
-
-    def phase_b(t, carry):
+            put(m, t, e * row(m, at))
+        yield
+        scatter(t)
+
+    def phase_b(t):
         at = span(t)
-        big_g[:, at] = dot(cat[...], hot_t[:, at])
+        big_g[:, at] = gather(t)
+        yield
         g0 = big_g[chan(0), at]
-        t1 = big_g[chan(1), at] * harm[1:2, at]
+        t1 = big_g[chan(1), at] * row(1, at)
         for m in range(2, 4):
-            t1 = t1 + big_g[chan(m), at] * harm[m : m + 1, at]
-        t2 = big_g[chan(4), at] * harm[4:5, at]
+            t1 = t1 + big_g[chan(m), at] * row(m, at)
+        t2 = big_g[chan(4), at] * row(4, at)
         for m in range(5, 9):
-            t2 = t2 + big_g[chan(m), at] * harm[m : m + 1, at]
+            t2 = t2 + big_g[chan(m), at] * row(m, at)
         t1_s[:, at] = t1
         t2_s[:, at] = t2
         v = v_s[:, at]
-        pre = latent(0, xh_s[:, at], xl_s[:, at], [v * g0, v * t1, v * t2])
+        high, low = spread_latent(xh_s[:, at], xl_s[:, at], [v * g0, v * t1, v * t2])
+        yield
+        pre = latent(0, high, low)
+        yield
         sg = sigmoid(pre)
         x = x_s[:, at] + pre * sg
         d1_s[:, at] = sg * (1.0 + pre * (1.0 - sg))
@@ -386,60 +443,74 @@
         x_s[:, at] = x
         xh_s[:, at] = xh
         xl_s[:, at] = xl
+        yield
         ge = dot(w_ge[...], jnp.concatenate([xh, xl, xh], 0))
+        yield
         g_s[:, at] = ge[0:C]
         e = ge[C:] * (env_scale * live_at(t))
         e1_s[:, at] = e
-        put(0, e)
+        put(0, t, e)
         for m in range(1, 9):
-            put(m, e * harm[m : m + 1, at])
-        acc[...] += scatter(t)
-        return carry
+            put(m, t, e * row(m, at))
+        yield
+        scatter(t)
 
     def path(i):
         return w_path[:, i : i + 1]
 
-    def phase_c(t, carry):
+    def phase_c(t):
         at = span(t)
-        big_h[:, at] = dot(cat[...], hot_t[:, at])
+        big_h[:, at] = gather(t)
+        yield
 
         def sums(low, high):
             a = big_g[chan(low), at] * big_h[chan(low), at]
-            b = big_h[chan(low), at] * harm[low : low + 1, at]
+            b = big_h[chan(low), at] * row(low, at)
             for m in range(low + 1, high):
                 h = big_h[chan(m), at]
                 a = a + big_g[chan(m), at] * h
-                b = b + h * harm[m : m + 1, at]
+                b = b + h * row(m, at)
             return a, b
 
         a1, b1 = sums(1, 4)
         a2, b2 = sums(4, 9)
         g0 = big_g[chan(0), at]
-        h0 = big_h[chan(0), at]
         c0 = path(0) * g0 + path(1) * t1_s[:, at] + path(2) * t2_s[:, at]
         h4 = path(4) * g0
         h6 = path(6) * g0
-        p0 = c0 * h0
+        p0 = c0 * big_h[chan(0), at]
         p1 = path(3) * a1 + h4 * b1
         p2 = path(5) * a2 + h6 * b2
-        v = v_s[:, at]
-        g = g_s[:, at]
-        gv = g * v
-        pre = latent(1, xh_s[:, at], xl_s[:, at], [gv * p0, gv * p1, gv * p2])
+        gv = g_s[:, at] * v_s[:, at]
+        high, low = spread_latent(xh_s[:, at], xl_s[:, at], [gv * p0, gv * p1, gv * p2])
+        yield
+        pre = latent(1, high, low)
+        yield
         sg = sigmoid(pre)
         x = x_s[:, at] + pre * sg
         d2 = sg * (1.0 + pre * (1.0 - sg))
-        hid = dot(w_fin[...], stacked(x))
+        x = stacked(x)
+        yield
+        hid = dot(w_fin[...], x)
+        yield
         sg = sigmoid(hid)
         live = live_at(t)
         ow = w_out[:, 0:1]
         eps_s[:, at] = jnp.sum(fold(ow * (hid * sg)), 0, keepdims=True) * live
         dhid = (ow * live) * (sg * (1.0 + hid * (1.0 - sg)))
-        dx = dot(w_finb[...], stacked(dhid))
-        dm = dot(w_latb[1], stacked(dx * d2))
+        dhid = stacked(dhid)
+        yield
+        dx = dot(w_finb[...], dhid)
+        yield
+        dpre = stacked(dx * d2)
+        yield
+        dm = dot(w_latb[1], dpre)
+        yield
         dx_s[:, at] = dx + dm[0:C]
         ds0, ds1, ds2 = dm[chan(1)], dm[chan(2)], dm[chan(3)]
         dgv = ds0 * p0 + ds1 * p1 + ds2 * p2
+        v = v_s[:, at]
+        g = g_s[:, at]
         dg_s[:, at] = dgv * v
         dv_s[:, at] = dgv * g
         u0 = ds0 * gv
@@ -453,37 +524,44 @@
         k2_s[:, at] = k2
         j1_s[:, at] = j1
         j2_s[:, at] = j2
-        uh = u0 * h0
+        uh = u0 * big_h[chan(0), at]
         dg0_s[:, at] = uh * path(0) + u1 * path(4) * b1 + u2 * path(6) * b2
         dt1_s[:, at] = uh * path(1)
         dt2_s[:, at] = uh * path(2)
-        put(0, u0 * c0)
+        put(0, t, u0 * c0)
         for m in range(1, 9):
             k, j = (k1, j1) if m < 4 else (k2, j2)
-            put(m, k * big_g[chan(m), at] + j * harm[m : m + 1, at])
-        acc[...] += scatter(t)
-        return carry
-
-    def phase_d(t, carry):
+            put(m, t, k * big_g[chan(m), at] + j * row(m, at))
+        yield
+        scatter(t)
+
+    def phase_d(t):
         at = span(t)
-        work[...] = dot(cat[...], hot_t[:, at])
-        de = work[chan(0), :]
+        wat = span(t % RING)
+        work[:, wat] = gather(t)
+        yield
+        de = work[chan(0), wat]
         for m in range(1, 9):
-            de = de + work[chan(m), :] * harm[m : m + 1, at]
+            de = de + work[chan(m), wat] * row(m, at)
         de = de * (env_scale * live_at(t))
         deh, del_ = halves(de)
         dgh, dgl = halves(dg_s[:, at])
-        dx = dx_s[:, at] + dot(
-            w_b1[...], jnp.concatenate([deh, dgh, del_, dgl, deh, dgh], 0)
-        )
-        dm = dot(w_latb[0], stacked(dx * d1_s[:, at]))
+        pair = jnp.concatenate([deh, dgh, del_, dgl, deh, dgh], 0)
+        yield
+        dx = dot(w_b1[...], pair)
+        yield
+        dx = dx_s[:, at] + dx
+        dpre = stacked(dx * d1_s[:, at])
+        yield
+        dm = dot(w_latb[0], dpre)
+        yield
         dx_s[:, at] = dx + dm[0:C]
         ds0, ds1, ds2 = dm[chan(1)], dm[chan(2)], dm[chan(3)]
         v = v_s[:, at]
         dv_s[:, at] += ds0 * big_g[chan(0), at] + ds1 * t1_s[:, at] + ds2 * t2_s[:, at]
         dt1 = dt1_s[:, at] + ds1 * v
         dt2 = dt2_s[:, at] + ds2 * v
-        put(0, dg0_s[:, at] + ds0 * v)
+        put(0, t, dg0_s[:, at] + ds0 * v)
         e = e1_s[:, at]
         for m in range(1, 9):
             if m < 4:
@@ -492,30 +570,37 @@
                 k, j, dt = k2_s[:, at], j2_s[:, at], dt2
             h = big_h[chan(m), at]
             dy_s[8 * m : 8 * m + 8, at] = fold(
-                j * h + dt * big_g[chan(m), at] + e * work[chan(m), :]
+                j * h + dt * big_g[chan(m), at] + e * work[chan(m), wat]
             )
-            put(m, k * h + dt * harm[m : m + 1, at])
-        acc[...] += scatter(t)
-        return carry
-
-    def phase_e(t, carry):
+            put(m, t, k * h + dt * row(m, at))
+        yield
+        scatter(t)
+
+    def phase_e(t):
         at = span(t)
-        work[...] = dot(cat[...], hot_t[:, at])
-        de = work[chan(0), :]
+        wat = span(t % RING)
+        work[:, wat] = gather(t)
+        yield
+        de = work[chan(0), wat]
         for m in range(1, 9):
-            de = de + work[chan(m), :] * harm[m : m + 1, at]
+            de = de + work[chan(m), wat] * row(m, at)
         de = de * (env_scale * live_at(t))
+        deh, del_ = halves(de)
+        dvh, dvl = halves(dv_s[:, at])
+        pair = jnp.concatenate([deh, dvh, del_, dvl, deh, dvh], 0)
         e = e0_s[:, at]
         dy = [None]
         for m in range(1, 9):
-            part = dy_s[8 * m : 8 * m + 8, at] + fold(e * work[chan(m), :])
+            part = dy_s[8 * m : 8 * m + 8, at] + fold(e * work[chan(m), wat])
             dy.append(jnp.sum(part, 0, keepdims=True))
-        deh, del_ = halves(de)
-        dvh, dvl = halves(dv_s[:, at])
-        dx = dx_s[:, at] + dot(
-            w_b0[...], jnp.concatenate([deh, dvh, del_, dvl, deh, dvh], 0)
-        )
-        dbasis = dot(w_embb[...], stacked(dx * d0_s[:, at]))
+        yield
+        dx = dot(w_b0[...], pair)
+        yield
+        dpre = jnp.concatenate(halves((dx_s[:, at] + dx) * d0_s[:, at]), 0)
+        yield
+        dbasis = dot(w_embb[...], dpre)
+        dbasis = dbasis[0:8] + dbasis[8:16]
+        yield
         drho = -jnp.sum(dbasis * basis_s[:, at], 0, keepdims=True)
         u = geo[0:3, at]
         rho = geo[3:4, at]
@@ -530,39 +615,45 @@
         first = hi(rows)
         rest = rows - first
         second = hi(rest)
-        acc_own[...] += dot(
-            jnp.concatenate([first, second, rest - second, jnp.zeros((4, T), f32)], 0).astype(bf16),
-            hot[at, :],
-        )
+        rows = jnp.concatenate(
+            [first, second, rest - second, jnp.zeros((4, T), f32)], 0
+        ).astype(bf16)
         s = slot_s[:, at]
         spread = jnp.concatenate([s * dd[c] for c in range(3)], 0)
         first = hi(spread)
-        acc_near[...] += dot_nt(
-            jnp.concatenate([first, spread - first], 0).astype(bf16), near[:, at]
-        )
-        return carry
-
-    acc[...] = jnp.zeros(acc.shape, f32)
-    lax.fori_loop(0, steps, phase_a, 0)
-    for phase in (phase_b, phase_c, phase_d):
+        spread = jnp.concatenate([first, spread - first], 0).astype(bf16)
+        yield
+        acc_own[...] += dot(rows, hot[at, :])
+        acc_near[...] += dot_nt(spread, near[:, at])
+
+    @pl.when(stage == 0)
+    def _():
+        run(phase_a)
         make_cat()
-        acc[...] = jnp.zeros(acc.shape, f32)
-        lax.fori_loop(0, steps, phase, 0)
-    make_cat()
-    acc_own[...] = jnp.zeros(acc_own.shape, f32)
-    acc_near[...] = jnp.zeros(acc_near.shape, f32)
-    lax.fori_loop(0, steps, phase_e, 0)
-
-    own = acc_own[0:4, :] + acc_own[4:8, :] + acc_own[8:12, :]
-    site_ref[...] = own[3:4, :]
-    ghosts = acc_near[0:96, :] + acc_near[96:192, :]
-    for c in range(3):
-        local = jnp.concatenate([ghosts[c * 32 : c * 32 + 1], ghosts[c * 32 + 1 : c * 32 + 2]], 1)
-        own_ref[c : c + 1, :] = local - own[c : c + 1]
-    ghost_ref[...] = jnp.zeros(ghost_ref.shape, f32)
-    for k in range(27):
+
+    for number, phase in ((1, phase_b), (2, phase_c), (3, phase_d)):
+
+        @pl.when(stage == number)
+        def _(phase=phase):
+            run(phase)
+            make_cat()
+
+    @pl.when(stage == 4)
+    def _():
+        acc_own[...] = jnp.zeros(acc_own.shape, f32)
+        acc_near[...] = jnp.zeros(acc_near.shape, f32)
+        run(phase_e)
+        own = acc_own[0:4, :] + acc_own[4:8, :] + acc_own[8:12, :]
+        site_ref[...] = own[3:4, :]
+        ghosts = acc_near[0:48, :] + acc_near[48:96, :]
         for c in range(3):
-            ghost_ref[k, c : c + 1, :] = ghosts[c * 32 + k + 2 : c * 32 + k + 3, :]
+            own_ref[c : c + 1, :] = ghosts[c * 16 : c * 16 + 1] - own[c : c + 1]
+        ghost_ref[...] = jnp.zeros(ghost_ref.shape, f32)
+        for k in range(27):
+            half = slice(k % 2 * 128, k % 2 * 128 + 128)
+            for c in range(3):
+                at = c * 16 + 1 + k // 2
+                ghost_ref[k, c : c + 1, :] = ghosts[at : at + 1, half]
 
 
 def pair_grads(table, positions, features, center, nbr, count, params):
@@ -583,17 +674,17 @@
         pltpu.VMEM((2, 256, 192), bf16),
         pltpu.VMEM((64, 384), bf16),
         pltpu.VMEM((64, 384), bf16),
-        pltpu.VMEM((8, 192), bf16),
+        pltpu.VMEM((16, 128), bf16),
         pltpu.VMEM((64, 8), f32),
         pltpu.VMEM((64, 8), f32),
-        pltpu.VMEM((29 * 64, 128), bf16),
-        pltpu.VMEM((96, 128), f32),
-        pltpu.VMEM((288, 128), bf16),
+        pltpu.VMEM((15 * 64, 256), bf16),
+        pltpu.VMEM((48, 256), f32),
+        pltpu.VMEM((144, 256), bf16),
         pltpu.VMEM((80, atoms), bf16),
         pltpu.VMEM((pairs, atoms), bf16),
         wide(2 * atoms, bf16),
-        wide(128, bf16),
-        wide(32),
+        wide(256, bf16),
+        wide(16),
         wide(8),
         wide(16),
         wide(8),
@@ -602,18 +693,17 @@
         wide(64, bf16),
     ]
     scratch += [wide(64)] * 18
-    scratch[-1] = wide(64)
     scratch += [wide(72), wide(1)]
     scratch += [
         wide(576),
         wide(576),
-        pltpu.VMEM((576, T), f32),
-        pltpu.VMEM((576, T), bf16),
-        pltpu.VMEM((576, T), bf16),
+        pltpu.VMEM((576, RING * T), f32),
+        pltpu.VMEM((576, RING * T), bf16),
+        pltpu.VMEM((576, RING * T), bf16),
         pltpu.VMEM((576, atoms), f32),
         pltpu.VMEM((576, 2 * atoms), bf16),
         pltpu.VMEM((16, atoms), f32),
-        pltpu.VMEM((192, 128), f32),
+        pltpu.VMEM((96, 256), f32),
     ]
     vmem = pl.BlockSpec(memory_space=pltpu.VMEM)
     return pl.pallas_call(
@@ -623,6 +713,7 @@
             jax.ShapeDtypeStruct((3, atoms), f32),
             jax.ShapeDtypeStruct((27, 8, 128), f32),
         ),
+        grid=(5,),
         in_specs=[vmem] * 14,
         out_specs=(vmem, vmem, vmem),
         scratch_shapes=scratch,

time: 120 us -> 77.6 us (0.65)
  Pallas kernels: 113 us -> 70.9 us
    pallas_call x1, Pallas kernels: 80.1 us -> 38.1 us  [pair_grads(): pl.pallas_call(pair_kernel, out_shape=(jax.ShapeDtypeStruct((1, atoms), f...]
where the time goes in v2:
time: 77.6 us; the launch traced here: 77.2 us
  Pallas kernels  70.9 us (91%)
  local copies, waits for them, and re-layouts  4.98 us (6%)
  between operations  1.34 us (2%)
    pallas_call x1, Pallas kernels, pair_grads(): pl.pallas_call(pair_kernel, out_shape=(jax.ShapeDtypeStruct((1, atoms), f...  38.1 us
    pallas_call x1, Pallas kernels, halo(): pl.pallas_call(halo_kernel, out_shape=jax.ShapeDtypeStruct((27, ROWS, sen...  21.2 us
    pallas_call x1, Pallas kernels, give_back(): pl.pallas_call(return_kernel, out_shape=jax.ShapeDtypeStruct(own_grad.sha...  11.6 us
    unnamed x6, local copies, waits for them, and re-layouts  4.98 us

profile of v2, /device:TPU:1, one launch (start us, length us, event | category | flops | bytes accessed | tf_op | source)
XLA Modules:
  0.0 77.2 jit_solution(16958047487636501924)
XLA Ops:
  0.6 0.0 copy-start
  1.3 1.3 %copy.17.path_ref = f32[2,7,64]{2,1,0:T(8,128)} copy(f32[2,7,64]{2,0,1:T(2,128)} %param.23) | data formatting | bytes 7168 | tf_op args[9]
  2.6 1.6 %copy.16.emb_ref = f32[136,64]{1,0:T(8,128)} copy(f32[136,64]{0,1:T(8,128)} %param.20) | data formatting | bytes 69632 | tf_op args[6]
  4.2 0.0 copy-done
  4.2 0.9 %copy.18.latent_ref = f32[2,256,64]{2,1,0:T(8,128)} copy(f32[2,256,64]{1,2,0:T(8,128)S(1)} %copy-done) | data formatting | bytes 262144 | tf_op args[10]
  5.0 21.2 %shard_map.149.table_ref = f32[27,72,128]{2,1,0:T(8,128)} custom-call(f32[3,256]{1,0:T(4,128)} %pos_ref.3, bf16[64,256]{1,0:T(8,128)(2,1)} %feat_ref.3, s32[1,128]{1,0:T(1,128)} %bitcast.7), custom_call_target="tpu_custom_call" | custom-call | tf_op jit(solution)/shard_map/pallas_call | solution.py:102
  26.3 38.1 %shard_map.150 = (f32[1,256]{1,0:T(1,128)}, f32[3,256]{1,0:T(4,128)}, f32[27,8,128]{2,1,0:T(8,128)}) custom-call(f32[27,72,128]{2,1,0:T(8,128)} %shard_map.149.table_ref, f32[3,256]{1,0:T(4,128)} %pos_ref.3, bf16[64,256]{1,0:T(8,128)(2,1)} %feat_ref.3, s32[1,3072]{1,0:T(1,128)} %bitcast.9, s32[1,3072]{1,0:T(1,128)} %bitcast.10, s32[1,1]{1,0:T(1,128)} %bitcast.6.count_ref, ...), custom_call_target="tpu_custom_call" | custom-call | flops 40000000000 | bytes 1000000 | tf_op jit(solution)/shard_map/pallas_call | solution.py:709
  64.4 11.6 %shard_map.151 = f32[3,256]{1,0:T(4,128)} custom-call(f32[27,8,128]{2,1,0:T(8,128)} %get-tuple-element.6.ghost_ref, f32[3,256]{1,0:T(4,128)} %get-tuple-element.7.own_ref, s32[1,128]{1,0:T(1,128)} %bitcast.8), custom_call_target="tpu_custom_call" | custom-call | tf_op jit(solution)/shard_map/pallas_call | solution.py:152
  76.0 1.3 %copy.21 = f32[3,256]{1,0:T(4,128)} copy(f32[3,256]{1,0:T(4,128)} %shard_map.151) | data formatting | bytes 6144
Async XLA Ops:
  0.6 3.6 %copy-start = (f32[2,256,64]{1,2,0:T(8,128)S(1)}, f32[2,256,64]{1,2,0:T(8,128)}, u32[]{:S(2)}) copy-start(f32[2,256,64]{1,2,0:T(8,128)} %param.24) | copy-start | bytes 393220

commit v3 on v2

--- a/solution.py
+++ b/solution.py
@@ -15,7 +15,8 @@
 f32 = jnp.float32
 bf16 = jnp.bfloat16
 C = 64
-SLOTS = [k for k in range(27) if k != 13]
+PLANE = [10, 12, 14, 16, 9, 11, 15, 17]
+NEAR = PLANE + [4, 22]
 ROWS = 72
 TILE = 256
 SKEW = 1
@@ -35,9 +36,9 @@
 
 def greet():
     barrier = pltpu.get_barrier_semaphore()
-    for k in SLOTS:
+    for k in NEAR:
         pl.semaphore_signal(barrier, inc=1, device_id=peer(k, 1), device_id_type=MESH)
-    pl.semaphore_wait(barrier, len(SLOTS))
+    pl.semaphore_wait(barrier, len(NEAR))
 
 
 def dot(a, b):
@@ -80,20 +81,28 @@
         + dot(parts[2].astype(bf16), pick)
     )
     send_buf[C + 3 : ROWS, :] = jnp.zeros((ROWS - C - 3, sent), f32)
-    copies = []
-    for k in SLOTS:
+    def send(source, k, to):
         copy = pltpu.make_async_remote_copy(
-            src_ref=send_buf,
+            src_ref=source,
             dst_ref=out_ref.at[k],
             send_sem=send_sem.at[k],
             recv_sem=recv_sem.at[k],
-            device_id=peer(k, -1),
+            device_id=peer(to, -1),
             device_id_type=MESH,
         )
         copy.start()
-        copies.append(copy)
+        return copy
+
+    plane = [send(send_buf, k, k) for k in PLANE]
+    later = [send(send_buf, k, k) for k in (4, 22)]
     out_ref[13] = jnp.zeros((ROWS, sent), f32)
-    for copy in copies:
+    for k, copy in zip(PLANE, plane):
+        copy.wait_recv()
+        later.append(send(out_ref.at[k], k - 9, 4))
+        later.append(send(out_ref.at[k], k + 9, 22))
+    for copy in plane:
+        copy.wait_send()
+    for copy in later:
         copy.wait()
 
 
@@ -113,31 +122,40 @@
     )(positions, features, rows)
 
 
-def return_kernel(ghost_ref, own_ref, rows_ref, force_ref, landed, send_sem, recv_sem):
+def return_kernel(ghost_ref, own_ref, rows_ref, force_ref, sides, plane, landed, send_sem, recv_sem):
     greet()
-    copies = []
-    for k in SLOTS:
+
+    def send(source, target, k, to):
         copy = pltpu.make_async_remote_copy(
-            src_ref=ghost_ref.at[k],
-            dst_ref=landed.at[k],
+            src_ref=source,
+            dst_ref=target,
             send_sem=send_sem.at[k],
             recv_sem=recv_sem.at[k],
-            device_id=peer(k, 1),
+            device_id=peer(to, 1),
             device_id_type=MESH,
         )
         copy.start()
-        copies.append(copy)
+        return copy
+
+    first = [
+        send(ghost_ref.at[0:9], sides.at[0], 4, 4),
+        send(ghost_ref.at[18:27], sides.at[1], 22, 22),
+    ]
     atoms = own_ref.shape[1]
     sent = rows_ref.shape[1]
     pick = (
         lax.broadcasted_iota(jnp.int32, (atoms, sent), 0)
         == jnp.broadcast_to(rows_ref[...], (atoms, sent))
     ).astype(bf16)
-    for copy in copies:
+    for copy in first:
         copy.wait()
-    owned = landed[SLOTS[0]]
-    for k in SLOTS[1:]:
-        owned = owned + landed[k]
+    plane[...] = ghost_ref[9:18] + sides[0] + sides[1]
+    second = [send(plane.at[k - 9], landed.at[k - 9], k, k) for k in PLANE]
+    owned = plane[4]
+    for copy in second:
+        copy.wait()
+    for k in PLANE:
+        owned = owned + landed[k - 9]
     parts = thirds(owned)
     back = (
         dot_nt(parts[0].astype(bf16), pick)
@@ -155,7 +173,9 @@
         in_specs=[pl.BlockSpec(memory_space=pltpu.VMEM)] * 3,
         out_specs=pl.BlockSpec(memory_space=pltpu.VMEM),
         scratch_shapes=[
-            pltpu.VMEM((27, 8, sent), f32),
+            pltpu.VMEM((2, 9, 8, sent), f32),
+            pltpu.VMEM((9, 8, sent), f32),
+            pltpu.VMEM((9, 8, sent), f32),
             pltpu.SemaphoreType.DMA((27,)),
             pltpu.SemaphoreType.DMA((27,)),
         ],
@@ -213,7 +233,7 @@
 
     @pl.when(stage == 0)
     def _():
-        emb = emb_ref[...]
+        emb = emb_ref[...].T
         emb_h = hi(emb)
         emb_l = emb - emb_h
         w_emb[...] = jnp.concatenate(
@@ -239,12 +259,12 @@
         w_finb[...] = backward_stack(final_ref[...])
         w_out[...] = jnp.broadcast_to(out_ref[...], (8, C)).T
         for layer in range(2):
-            cols = jnp.concatenate([path_ref[layer], jnp.ones((1, C), f32)], 0).T
+            cols = jnp.concatenate([path_ref[:, layer], jnp.ones((1, C), f32)], 0).T
             if layer == 0:
                 w_path[...] = cols
+            mix = latent_ref[layer].T
             scaled = jnp.concatenate(
-                [latent_ref[layer, 0:C]]
-                + [latent_ref[layer, chan(i + 1)] * cols[:, i : i + 1] for i in range(3)],
+                [mix[0:C]] + [mix[chan(i + 1)] * cols[:, i : i + 1] for i in range(3)],
                 0,
             )
             first = hi(scaled)
@@ -660,6 +680,8 @@
     pairs = center.shape[1]
     atoms = positions.shape[1]
     T = TILE
+    emb, value, env, path, latent, *rest = params
+    params = (emb.T, value, env, path.transpose(1, 0, 2), latent.transpose(0, 2, 1), *rest)
 
     def wide(rows, dtype=f32):
         return pltpu.VMEM((rows, pairs), dtype)

time: 77.6 us -> 71.7 us (0.924)
  local copies, waits for them, and re-layouts: 4.98 us -> 1.27 us
  Pallas kernels: 70.9 us -> 68.7 us
    unnamed x6 -> x1, local copies, waits for them, and re-layouts: 4.98 us -> 1.27 us
    pallas_call x1, Pallas kernels: 11.6 us -> 9.82 us  [give_back(): pl.pallas_call(return_kernel, out_shape=jax.ShapeDtypeStruct(own_grad.sha...]
where the time goes in v3:
time: 71.7 us; the launch traced here: 71.2 us
  Pallas kernels  68.7 us (96%)
  between operations  1.29 us (2%)
  local copies, waits for them, and re-layouts  1.27 us (2%)
    pallas_call x1, Pallas kernels, pair_grads(): pl.pallas_call(pair_kernel, out_shape=(jax.ShapeDtypeStruct((1, atoms), f...  38.2 us
    pallas_call x1, Pallas kernels, halo(): pl.pallas_call(halo_kernel, out_shape=jax.ShapeDtypeStruct((27, ROWS, sen...  20.6 us
    pallas_call x1, Pallas kernels, give_back(): pl.pallas_call(return_kernel, out_shape=jax.ShapeDtypeStruct(own_grad.sha...  9.82 us

profile of v3, /device:TPU:1, one launch (start us, length us, event | category | flops | bytes accessed | tf_op | source)
XLA Modules:
  0.0 71.2 jit_solution(1088680974678911532)
XLA Ops:
  1.3 20.6 %shard_map.149.table_ref = f32[27,72,128]{2,1,0:T(8,128)} custom-call(f32[3,256]{1,0:T(4,128)} %pos_ref.3, bf16[64,256]{1,0:T(8,128)(2,1)} %feat_ref.3, s32[1,128]{1,0:T(1,128)} %bitcast.10), custom_call_target="tpu_custom_call" | custom-call | tf_op jit(solution)/shard_map/pallas_call | solution.py:111
  21.9 38.2 %shard_map.150 = (f32[1,256]{1,0:T(1,128)}, f32[3,256]{1,0:T(4,128)}, f32[27,8,128]{2,1,0:T(8,128)}) custom-call(f32[27,72,128]{2,1,0:T(8,128)} %shard_map.149.table_ref, f32[3,256]{1,0:T(4,128)} %pos_ref.3, bf16[64,256]{1,0:T(8,128)(2,1)} %feat_ref.3, s32[1,3072]{1,0:T(1,128)} %bitcast.14, s32[1,3072]{1,0:T(1,128)} %bitcast.15, s32[1,1]{1,0:T(1,128)} %bitcast.9.count_ref, ...), custom_call_target="tpu_custom_call" | custom-call | flops 40000000000 | bytes 1000000 | tf_op jit(solution)/shard_map/pallas_call | solution.py:731
  60.1 9.8 %shard_map.151 = f32[3,256]{1,0:T(4,128)} custom-call(f32[27,8,128]{2,1,0:T(8,128)} %get-tuple-element.6.ghost_ref, f32[3,256]{1,0:T(4,128)} %get-tuple-element.7.own_ref, s32[1,128]{1,0:T(1,128)} %bitcast.11), custom_call_target="tpu_custom_call" | custom-call | tf_op jit(solution)/shard_map/pallas_call | solution.py:170
  70.0 1.3 %copy.18 = f32[3,256]{1,0:T(4,128)} copy(f32[3,256]{1,0:T(4,128)} %shard_map.151) | data formatting | bytes 6144

commit v4 on v3

--- a/solution.py
+++ b/solution.py
@@ -20,7 +20,7 @@
 ROWS = 72
 TILE = 256
 SKEW = 1
-GROUP = 3
+GROUP = 2
 RING = 6
 
 

time: 71.7 us -> 70.8 us (0.987)
  Pallas kernels: 68.7 us -> 67.7 us
    pallas_call x1, Pallas kernels: 38.2 us -> 37.2 us  [pair_grads(): pl.pallas_call(pair_kernel, out_shape=(jax.ShapeDtypeStruct((1, atoms), f...]
where the time goes in v4:
time: 70.8 us; the launch traced here: 70.3 us
  Pallas kernels  67.7 us (96%)
  between operations  1.29 us (2%)
  local copies, waits for them, and re-layouts  1.27 us (2%)
    pallas_call x1, Pallas kernels, pair_grads(): pl.pallas_call(pair_kernel, out_shape=(jax.ShapeDtypeStruct((1, atoms), f...  37.2 us
    pallas_call x1, Pallas kernels, halo(): pl.pallas_call(halo_kernel, out_shape=jax.ShapeDtypeStruct((27, ROWS, sen...  20.6 us
    pallas_call x1, Pallas kernels, give_back(): pl.pallas_call(return_kernel, out_shape=jax.ShapeDtypeStruct(own_grad.sha...  9.81 us

profile of v4, /device:TPU:1, one launch (start us, length us, event | category | flops | bytes accessed | tf_op | source)
XLA Modules:
  0.0 70.3 jit_solution(9750212063436286349)
XLA Ops:
  1.3 20.6 %shard_map.149.table_ref = f32[27,72,128]{2,1,0:T(8,128)} custom-call(f32[3,256]{1,0:T(4,128)} %pos_ref.3, bf16[64,256]{1,0:T(8,128)(2,1)} %feat_ref.3, s32[1,128]{1,0:T(1,128)} %bitcast.10), custom_call_target="tpu_custom_call" | custom-call | tf_op jit(solution)/shard_map/pallas_call | solution.py:111
  21.9 37.2 %shard_map.150 = (f32[1,256]{1,0:T(1,128)}, f32[3,256]{1,0:T(4,128)}, f32[27,8,128]{2,1,0:T(8,128)}) custom-call(f32[27,72,128]{2,1,0:T(8,128)} %shard_map.149.table_ref, f32[3,256]{1,0:T(4,128)} %pos_ref.3, bf16[64,256]{1,0:T(8,128)(2,1)} %feat_ref.3, s32[1,3072]{1,0:T(1,128)} %bitcast.14, s32[1,3072]{1,0:T(1,128)} %bitcast.15, s32[1,1]{1,0:T(1,128)} %bitcast.9.count_ref, ...), custom_call_target="tpu_custom_call" | custom-call | flops 40000000000 | bytes 1000000 | tf_op jit(solution)/shard_map/pallas_call | solution.py:731
  59.2 9.8 %shard_map.151 = f32[3,256]{1,0:T(4,128)} custom-call(f32[27,8,128]{2,1,0:T(8,128)} %get-tuple-element.6.ghost_ref, f32[3,256]{1,0:T(4,128)} %get-tuple-element.7.own_ref, s32[1,128]{1,0:T(1,128)} %bitcast.11), custom_call_target="tpu_custom_call" | custom-call | tf_op jit(solution)/shard_map/pallas_call | solution.py:170
  69.0 1.3 %copy.18 = f32[3,256]{1,0:T(4,128)} copy(f32[3,256]{1,0:T(4,128)} %shard_map.151) | data formatting | bytes 6144
